TPU v7x, 256 devices: a whole 4x4x8 slice. The times are simulated.
256 devices in a mesh: tile: 64 (over z, y, core), pair: 4 (over x).
Axes of the slice: x: 4, y: 4, z: 8, core: 2. Of those that a mesh axis runs over, the one named last changes fastest.
Arguments:
- slc: bfloat16 [128, 128, 2, 8192], P('tile'), may hold values from -64 to 64
- pairs: int32 [384, 2], replicated, may hold values from 0 to 127, as said below
- groups: int32 [384, 1], replicated, may hold values from 0 to 3; in each aligned block of 384 rows (0 to 383, 384 to 767, ...) at most 192 rows name the same one
- tile_source: int32 [128], replicated, may hold values from 0 to 127, each once
Outputs:
- rhs: float32 [128, 128, 2, 128], P('pair', 'tile')
- coherence: float32 [768, 128, 128], P('pair', 'tile')
Inputs may be any that keep to these rules, and one draw needn't show every extreme that they name: `pairs`: every row holds two different epochs, the smaller first, and every epoch appears in some row. `groups`: at most 192 pairs belong to one group, and one group has exactly 192.
All inputs are finite; a program needn't handle non-finite values.
Results may differ from a plain program's by a relative error of at most 0.0003.
Values may be sent and summed in bfloat16 or wider, within the bound.
No kernel may reach another device: no remote copies, remote signals or barrier semaphores. Data moves between devices by JAX's collectives and lax.ppermute only.
A program may use at most 128 MiB of HBM per device.

v0:
```python
import jax
import jax.numpy as jnp
from jax import lax
from jax.sharding import PartitionSpec as P

TR = 512


EPS = 1e-06


def box_means(values):
    lead = values.shape[:-1]
    pixels = values.shape[-1]
    lines = pixels // TR
    grid = values.reshape(lead + (lines // 4, 4, TR // 16, 16))
    return (jnp.sum(grid, axis=(-3, -1)) * (1.0 / 64.0)).reshape(lead + (pixels // 64,))


def pair_terms(data, refs, secs, live):
    n_epochs, count, _, pixels = data.shape
    looks = pixels // 64
    width = refs.shape[0]
    ref_data = jnp.take(data, refs, axis=0)
    sec_data = jnp.take(data, secs, axis=0)
    a_re = ref_data[:, :, 0].astype(jnp.float32)
    a_im = ref_data[:, :, 1].astype(jnp.float32)
    b_re = sec_data[:, :, 0].astype(jnp.float32)
    b_im = sec_data[:, :, 1].astype(jnp.float32)
    inter_re = box_means(a_re * b_re + a_im * b_im)
    inter_im = box_means(a_im * b_re - a_re * b_im)
    d_re = data[:, :, 0].astype(jnp.float32)
    d_im = data[:, :, 1].astype(jnp.float32)
    level = box_means(d_re * d_re + d_im * d_im)
    scale = lax.rsqrt(jnp.take(level, refs, axis=0) + EPS) * lax.rsqrt(
        jnp.take(level, secs, axis=0) + EPS
    )
    gamma_re = inter_re * scale
    gamma_im = inter_im * scale
    weight = (gamma_re * gamma_re + gamma_im * gamma_im) * live.astype(jnp.float32)[:, None, None]
    weighted = jnp.stack([weight * gamma_re, weight * gamma_im], axis=2)
    epochs = jnp.arange(n_epochs, dtype=jnp.int32)[:, None]
    incidence = (epochs == secs[None, :]).astype(jnp.float32) - (epochs == refs[None, :]).astype(
        jnp.float32
    )
    partial_rhs = jnp.dot(
        incidence,
        weighted.reshape(width, -1),
        precision=lax.Precision.HIGHEST,
        preferred_element_type=jnp.float32,
    )
    return (weight, partial_rhs.reshape(n_epochs, count, 2, looks))


def local(slc, pairs, groups, tile_source):
    n_tile = lax.axis_size("tile")
    e_dev, n_tiles, _, pixels = slc.shape
    tiles_dev = n_tiles // n_tile
    n_pairs = pairs.shape[0]
    capacity = n_pairs // 2
    member = lax.axis_index("pair")
    pair_ids = jnp.arange(n_pairs, dtype=jnp.int32)
    ordered = jnp.take(slc, tile_source, axis=1).reshape(e_dev, n_tile, tiles_dev, 2, pixels)
    mine = groups[:, 0] == member
    rank = jnp.cumsum(mine.astype(jnp.int32)) - 1
    slot_hit = mine[None, :] & (rank[None, :] == jnp.arange(capacity, dtype=jnp.int32)[:, None])
    slot_pair = jnp.sum(jnp.where(slot_hit, pair_ids[None, :], 0), axis=1)
    slot_live = jnp.any(slot_hit, axis=1)
    refs = jnp.take(pairs[:, 0], slot_pair)
    secs = jnp.take(pairs[:, 1], slot_pair)
    weight, partial_rhs = pair_terms(
        lax.all_to_all(ordered, "tile", split_axis=1, concat_axis=0, tiled=True)[:, 0],
        refs,
        secs,
        slot_live,
    )
    rhs = lax.psum_scatter(partial_rhs, "pair", scatter_dimension=0, tiled=True)
    return (rhs, weight)


def solution(mesh):
    placed = (P("tile", None, None, None), P(), P(), P())
    return jax.shard_map(
        local,
        mesh=mesh,
        in_specs=placed,
        out_specs=(P("pair", "tile", None, None), P("pair", "tile", None)),
        check_vma=False,
    )
```

profile of v0, /device:TPU:8, one launch (start us, length us, event | category | flops | bytes accessed | tf_op | source)
XLA Modules:
  0.0 510.6 jit_solution(2269682149431686864)
XLA Ops:
  8.6 23.2 %gather_fusion = bf16[128,2,2,8192]{3,2,1,0:T(2,128)(2,1)} fusion(bf16[2,128,2,8192]{3,2,1,0:T(2,128)(2,1)} %param.10, s32[1024]{0:T(1024)S(1)} %pad_clamp_fusion.2), kind=kCustom, calls=%fused_computation.6 | custom fusion | bytes 16777728 | tf_op jit(solution)/shard_map/jit(_take)/gather | solution.py:63
  31.9 10.9 %broadcast_select_fusion = bf16[2,64,2,2,8192]{4,3,2,0,1:T(2,128)(2,1)} fusion(pred[64,2]{1,0:T(8,128)(4,1)S(1)} %broadcast_in_dim.60, bf16[2,64,2,2,8192]{4,3,0,2,1:T(2,128)(2,1)} %bitcast.31), kind=kLoop, calls=%fused_computation.7 | loop fusion | flops 4194304 | bytes 16777344 | tf_op jit(solution)/shard_map/jit(_take)/select_n | solution.py:63
  42.8 12.4 %all-to-all-start = ((bf16[2,64,2,2,8192]{4,3,2,0,1:T(2,128)(2,1)}), bf16[2,64,2,2,8192]{4,3,2,0,1:T(2,128)(2,1)}, u32[]{:S(2)}, u32[]{:S(2)}) async-start(bf16[2,64,2,2,8192]{4,3,2,0,1:T(2,128)(2,1)} %broadcast_select_fusion), calls=%async_computation | async-start | bytes 16777216 | tf_op jit(solution)/shard_map/all_to_all | solution.py:72
  56.3 1.6 gather_fusion.2
  57.9 1.6 gather_fusion.1
  59.6 180.7 %all-to-all-done = bf16[2,64,2,2,8192]{4,3,2,0,1:T(2,128)(2,1)} async-done(((bf16[2,64,2,2,8192]{4,3,2,0,1:T(2,128)(2,1)}), bf16[2,64,2,2,8192]{4,3,2,0,1:T(2,128)(2,1)}, u32[]{:S(2)}, u32[]{:S(2)}) %all-to-all-start) | async-done | bytes 8388640 | tf_op jit(solution)/shard_map/all_to_all | solution.py:72
  240.2 26.7 %fusion.17 = (bf16[128,2,1,8192]{3,2,1,0:T(2,128)(2,1)}, bf16[128,2,1,8192]{3,2,1,0:T(2,128)(2,1)}) fusion(bf16[128,2,2,8192]{3,2,1,0:T(2,128)(2,1)} %bitcast.7), kind=kLoop, calls=%fused_computation.64 | loop fusion | bytes 16777216 | tf_op jit(solution)/shard_map/slice | solution.py:32
  266.9 32.3 %gather_fusion.4 = bf16[192,2,2,8192]{3,2,1,0:T(2,128)(2,1)} fusion(bf16[128,2,2,8192]{3,2,1,0:T(2,128)(2,1)} %bitcast.7, s32[1024]{0:T(1024)S(1)} %pad_clamp_fusion), kind=kCustom, calls=%fused_computation.4.clone | custom fusion | bytes 25166592 | tf_op jit(solution)/shard_map/jit(_take)/gather | solution.py:25
  299.2 32.3 %gather_fusion.3 = bf16[192,2,2,8192]{3,2,1,0:T(2,128)(2,1)} fusion(bf16[128,2,2,8192]{3,2,1,0:T(2,128)(2,1)} %bitcast.7, s32[1024]{0:T(1024)S(1)} %pad_clamp_fusion.1), kind=kCustom, calls=%fused_computation.1.clone | custom fusion | bytes 25166592 | tf_op jit(solution)/shard_map/jit(_take)/gather | solution.py:24
  331.5 22.8 %multiply_add_fusion = f32[128,2,1,8192]{3,0,2,1:T(8,128)} fusion(bf16[128,2,1,8192]{3,2,1,0:T(2,128)(2,1)} %get-tuple-element.29, bf16[128,2,1,8192]{3,2,1,0:T(2,128)(2,1)} %get-tuple-element.28), kind=kLoop, calls=%fused_computation.16 | loop fusion | flops 10485760 | bytes 16777216 | tf_op jit(solution)/shard_map/add | solution.py:34
  354.2 8.8 %copy.56 = f32[128,2,1,8192]{0,3,1,2:T(8,128)} copy(f32[128,2,1,8192]{3,0,2,1:T(8,128)} %multiply_add_fusion) | data formatting | bytes 16777216 | tf_op jit(solution)/shard_map/add | solution.py:34
  363.1 4.2 reduce_sum.38
  367.4 0.9 gather_fusion.6
  368.3 0.9 gather_fusion.5
  369.2 48.1 %copy_select_fusion = (bf16[192,2,2,8192]{3,0,2,1:T(8,128)(2,1)S(1)}, bf16[192,2,2,8192]{3,0,2,1:T(8,128)(2,1)}) fusion(bf16[192,2,2,8192]{3,2,1,0:T(2,128)(2,1)} %gather_fusion.4, pred[192]{0:T(512)(128)(4,1)S(1)} %get-tuple-element.30, bf16[192,2,2,8192]{3,2,1,0:T(2,128)(2,1)} %gather_fusion.3, pred[192]{0:T(512)(128)(4,1)S(1)} %get-tuple-element.22), kind=kLoop, calls=%fused_computation.14 | loop fusion | flops 12582912 | bytes 50332032 | tf_op jit(solution)/shard_map/jit(_take)/select_n | solution.py:25
  417.2 13.8 %fusion.1 = (f32[192,2,1,8192]{3,0,2,1:T(8,128)}, f32[192,2,1,8192]{3,0,2,1:T(8,128)}) fusion(bf16[192,2,2,8192]{3,0,2,1:T(8,128)(2,1)S(1)} %get-tuple-element.32, bf16[192,2,2,8192]{3,0,2,1:T(8,128)(2,1)} %get-tuple-element.33), kind=kLoop, calls=%fused_computation.13 | loop fusion | flops 31457280 | bytes 50331648 | tf_op jit(solution)/shard_map/sub | solution.py:31
  431.0 14.9 %copy.60 = f32[192,2,1,8192]{0,3,1,2:T(8,128)} copy(f32[192,2,1,8192]{3,0,2,1:T(8,128)} %get-tuple-element.26) | data formatting | bytes 25165824 | tf_op jit(solution)/shard_map/sub | solution.py:31
  445.9 8.4 %reduce_sum.39 = f32[192,2,4,32]{0,3,2,1:T(8,128)S(1)} reduce(f32[192,2,4,4,32,16]{0,5,4,3,2,1:T(8,128)} %bitcast.30, f32[]{:T(128)} %constant.47.clone.1), dimensions={3,5}, to_apply=%region_5.9 | reduce | flops 3096576 | bytes 12779524 | tf_op jit(solution)/shard_map/reduce_sum | solution.py:17
  454.6 14.7 %copy.53 = f32[192,2,1,8192]{0,3,1,2:T(8,128)} copy(f32[192,2,1,8192]{3,0,2,1:T(8,128)} %get-tuple-element.27) | data formatting | bytes 25165824 | tf_op jit(solution)/shard_map/add | solution.py:30
  469.3 8.4 %reduce_sum.37 = f32[192,2,4,32]{0,3,2,1:T(8,128)S(1)} reduce(f32[192,2,4,4,32,16]{0,5,4,3,2,1:T(8,128)} %bitcast.29, f32[]{:T(128)} %constant.47.clone.1), dimensions={3,5}, to_apply=%region_3.6 | reduce | flops 3096576 | bytes 12779524 | tf_op jit(solution)/shard_map/reduce_sum | solution.py:17
  477.9 1.4 multiply_bitcast_fusion.1
  480.6 1.2 fusion.2
  481.8 20.2 %reduce-scatter.2.cloned.1.call-done = f32[32,2,2,128]{3,0,2,1:T(8,128)} async-done(((f32[128,2,2,128]{3,0,2,1:T(8,128)}), f32[32,2,2,128]{3,0,2,1:T(8,128)}) %reduce-scatter.2.cloned.1.call-update) | async-done | bytes 65552 | tf_op jit(solution)/shard_map/reduce_scatter | solution.py:77
  502.0 1.5 copy.64
  (41 shorter events, 4.2 us)
Async XLA Ops:
  42.7 12.5 %copy-start.1 = (s32[384,1]{0,1:T(1,128)S(1)}, s32[384,1]{0,1:T(1,128)}, u32[]{:S(2)}) copy-start(s32[384,1]{0,1:T(1,128)} %param.12) | copy-start | bytes 4612
  42.7 13.5 %copy-start.2 = (s32[384,2]{0,1:T(2,128)S(1)}, s32[384,2]{0,1:T(2,128)}, u32[]{:S(2)}) copy-start(s32[384,2]{0,1:T(2,128)} %param.11) | copy-start | bytes 9220
  42.8 197.5 %all-to-all-start = ((bf16[2,64,2,2,8192]{4,3,2,0,1:T(2,128)(2,1)}), bf16[2,64,2,2,8192]{4,3,2,0,1:T(2,128)(2,1)}, u32[]{:S(2)}, u32[]{:S(2)}) async-start(bf16[2,64,2,2,8192]{4,3,2,0,1:T(2,128)(2,1)} %broadcast_select_fusion), calls=%async_computation | async-start | bytes 16777216 | tf_op jit(solution)/shard_map/all_to_all | solution.py:72
  55.2 446.8 %reduce-scatter.2.cloned.1.call-start = ((), (), s32[]{:S(2)}) async-start(), calls=%async_computation.2 | async-start | bytes 327680 | tf_op jit(solution)/shard_map/reduce_scatter | solution.py:77
  479.4 24.2 %copy-start = (f32[192,2,128]{2,1,0:T(2,128)}, f32[192,2,128]{2,1,0:T(2,128)S(1)}, u32[]{:S(2)}) copy-start(f32[192,2,128]{2,1,0:T(2,128)S(1)} %get-tuple-element.20) | copy-start | bytes 589828
Sparse Core Ops, SparseCore 0:
  481.9 19.9 reduce-scatter.1
where the time goes:
time: 520 us; the launch traced here: 511 us
  waiting for transfers between devices  201 us (39%)
  local copies, waits for them, and re-layouts  161 us (31%)
  other arithmetic  121 us (23%)
  between operations  14.5 us (3%)
  starting transfers between devices  12.5 us (2%)
    all_to_all x1, waiting for transfers between devices, local(): lax.all_to_all(ordered, 'tile', split_axis=1, concat_axis=0, tiled=True)  181 us
    select_n x2, other arithmetic, pair_terms(): sec_data = jnp.take(data, secs, axis=0)  48.1 us
    gather x1, local copies, waits for them, and re-layouts, pair_terms(): ref_data = jnp.take(data, refs, axis=0)  32.3 us
    gather x1, local copies, waits for them, and re-layouts, pair_terms(): sec_data = jnp.take(data, secs, axis=0)  32.3 us
    slice x1, local copies, waits for them, and re-layouts, pair_terms(): d_re = data[:, :, 0].astype(jnp.float32)  26.7 us
    gather x1, local copies, waits for them, and re-layouts, local(): jnp.take(slc, tile_source, axis=1)  23.2 us
    add x1, other arithmetic, pair_terms(): level = box_means(d_re * d_re + d_im * d_im)  22.8 us
    reduce_sum x3, other arithmetic, box_means(): jnp.sum(grid, axis=(-3, -1)) * (1.0 / 64.0)  21.1 us
  transfers between devices with their start and end apart: 2, of which 2 were waited for; matrix products, arithmetic and copies ran while one was open for 1% of the time, Pallas kernels for 0%

commit v1 on v0

v1 whole, which is shorter than its diff:
```python
import functools

import jax
import jax.numpy as jnp
from jax import lax
from jax.experimental import pallas as pl
from jax.experimental.pallas import tpu as pltpu
from jax.sharding import PartitionSpec as P

EPS = 1e-06
LOOK_PIXELS = 64
LANES = 128
BATCH = 8


def split_dot(ones, x):
    high = x.astype(jnp.bfloat16)
    rest = x - high.astype(jnp.float32)
    middle = rest.astype(jnp.bfloat16)
    low = (rest - middle.astype(jnp.float32)).astype(jnp.bfloat16)
    width = x.shape[1]
    out = jnp.dot(ones, jnp.concatenate([high, middle, low], axis=1), preferred_element_type=jnp.float32)
    return out[:, :width] + out[:, width : 2 * width] + out[:, 2 * width :]


def dot_split(x, ones):
    high = x.astype(jnp.bfloat16)
    rest = x - high.astype(jnp.float32)
    middle = rest.astype(jnp.bfloat16)
    low = (rest - middle.astype(jnp.float32)).astype(jnp.bfloat16)
    rows = x.shape[0]
    out = jnp.dot(jnp.concatenate([high, middle, low], axis=0), ones, preferred_element_type=jnp.float32)
    return out[:rows] + out[rows : 2 * rows] + out[2 * rows :]


def order_kernel(source_ref, slc_ref, out_ref, sem):
    n_dev, _, tiles_dev, _, part = out_ref.shape
    start = pl.multiple_of(lax.axis_index("pair") * part, part)

    @pl.loop(0, n_dev)
    def _(d):
        for k in range(tiles_dev):
            src = source_ref[d * tiles_dev + k]
            pltpu.make_async_copy(
                slc_ref.at[:, src, :, pl.ds(start, part)], out_ref.at[d, :, k], sem
            ).start()

    pltpu.make_async_copy(out_ref, out_ref, sem).wait()


def lane_bit(bit):
    return (lax.broadcasted_iota(jnp.int32, (8, LANES), 1) & bit) == 0


def terms_kernel(pairs_sm, data_ref, pairs_ref, groups_ref, out_ref, wide, norm, gamma):
    n_epochs = data_ref.shape[0]
    n_pairs = pairs_ref.shape[1]
    step = wide.shape[0]
    sub = lax.broadcasted_iota(jnp.int32, (8, LANES), 0)
    lane = lax.broadcasted_iota(jnp.int32, (8, LANES), 1)
    first = sub < 4
    rows_i = lax.broadcasted_iota(jnp.int32, (LANES, LANES), 0)
    cols_i = lax.broadcasted_iota(jnp.int32, (LANES, LANES), 1)
    same_look = (rows_i // 16 == cols_i // 16).astype(jnp.bfloat16)

    @pl.loop(0, n_epochs // step)
    def _(block):
        at = pl.ds(block * step, step)
        wide[...] = data_ref[at].astype(jnp.float32)
        re = wide[:, :, pl.ds(0, 16, stride=2), :]
        im = wide[:, :, pl.ds(1, 16, stride=2), :]
        power = re * re + im * im
        lines = power[:, :, 0:8] + power[:, :, 8:16]
        lines = lines + pltpu.roll(lines, 4, 2)
        level = dot_split(lines.reshape(step * 2 * 8, LANES), same_look).reshape(step, 2, 8, LANES)
        inv = lax.rsqrt(level * (1.0 / LOOK_PIXELS) + EPS) * 0.125
        inv = jnp.concatenate([inv, inv], axis=2)
        norm[at, 0] = re * inv
        norm[at, 1] = im * inv

    @pl.loop(0, n_pairs // BATCH)
    def _(batch):
        def one(j):
            q = batch * BATCH + j
            r = pairs_sm[0, q]
            t = pairs_sm[1, q]
            a_re, a_im = norm[r, 0], norm[r, 1]
            b_re, b_im = norm[t, 0], norm[t, 1]
            parts = []
            for cross in (a_re * b_re + a_im * b_im, a_im * b_re - a_re * b_im):
                s0 = cross[0, 0:8] + cross[0, 8:16]
                s1 = cross[1, 0:8] + cross[1, 8:16]
                parts.append(jnp.where(first, s0, s1) + pltpu.roll(jnp.where(first, s1, s0), 4, 0))
            return merge(parts[0], parts[1], 8)

        def merge(a, b, k):
            return jnp.where(
                (lane & k) == 0, a + pltpu.roll(a, LANES - k, 1), b + pltpu.roll(b, k, 1)
            )

        def tree(js, k):
            if len(js) == 1:
                return one(js[0])
            return merge(tree([j for j in js if not j & k], k // 2), tree([j for j in js if j & k], k // 2), k)

        z = tree(list(range(BATCH)), 4)
        for k in (4, 2, 1):
            up = pltpu.roll(pltpu.roll(z, k, 1), 8 - k, 0)
            down = pltpu.roll(pltpu.roll(z, LANES - k, 1), k, 0)
            low_row, low_lane = (sub & k) == 0, (lane & k) == 0
            z = jnp.where(low_row == low_lane, z, jnp.where(low_row, up, down))
        gamma[pl.ds(pl.multiple_of(batch * BATCH, BATCH), BATCH), :] = z

    z = gamma[...]
    comp0 = (lax.broadcasted_iota(jnp.int32, z.shape, 1) & 8) == 0
    square = z * z
    weight = square + jnp.where(comp0, pltpu.roll(square, LANES - 8, 1), pltpu.roll(square, 8, 1))
    refs, secs, groups = pairs_ref[0:1, :], pairs_ref[1:2, :], groups_ref[0:1, :]
    epochs = lax.broadcasted_iota(jnp.int32, (n_epochs, n_pairs), 0)
    incidence = (epochs == secs).astype(jnp.float32) - (epochs == refs).astype(jnp.float32)
    rhs = split_dot(incidence.astype(jnp.bfloat16), weight * z)

    n_groups = out_ref.shape[0]
    mine = (lax.broadcasted_iota(jnp.int32, (8, n_pairs), 0) == groups).astype(jnp.float32)
    before = (
        lax.broadcasted_iota(jnp.int32, (n_pairs, n_pairs), 0)
        < lax.broadcasted_iota(jnp.int32, (n_pairs, n_pairs), 1)
    )
    ranks = jnp.dot(
        mine.astype(jnp.bfloat16), before.astype(jnp.bfloat16), preferred_element_type=jnp.float32
    )
    rank = jnp.sum(mine * ranks, axis=0, keepdims=True).astype(jnp.int32)
    half = n_pairs // 4
    slot = jnp.where(rank < half, groups * half + rank, n_pairs + groups * half + rank - half)
    hit = (lax.broadcasted_iota(jnp.int32, (2 * n_pairs, n_pairs), 0) == slot).astype(jnp.bfloat16)
    chosen = split_dot(hit, weight)
    chosen = jnp.where(comp0, chosen[:n_pairs], chosen[n_pairs:])
    e_out = n_epochs // n_groups
    for g in range(n_groups):
        out_ref[g, 0:half, :] = chosen[g * half : (g + 1) * half]
        out_ref[g, half : half + e_out, :] = rhs[g * e_out : (g + 1) * e_out]


def place_kernel(parts_ref, rhs_ref, coherence_ref):
    n_parts, rows, _ = parts_ref.shape
    half = coherence_ref.shape[0] // 2
    i = lax.broadcasted_iota(jnp.int32, (LANES, LANES), 0)
    j = lax.broadcasted_iota(jnp.int32, (LANES, LANES), 1)
    total = [[None, None], [None, None]]
    for q in range(n_parts):
        ones = []
        for comp in range(2):
            for slot in range(2):
                look = q * 32 + (i & 3) * 8 + i // 16
                ones.append(
                    ((j == look) & (((i // 8) & 1) == comp) & (((i // 4) & 1) == slot)).astype(jnp.bfloat16)
                )
        out = dot_split(parts_ref[q], jnp.concatenate(ones, axis=1))
        for comp in range(2):
            for slot in range(2):
                k = comp * 2 + slot
                piece = out[:, k * LANES : (k + 1) * LANES]
                total[comp][slot] = piece if q == 0 else total[comp][slot] + piece
    for comp in range(2):
        for slot in range(2):
            coherence_ref[pl.ds(comp * half, half), slot, :] = total[comp][slot][:half]
            rhs_ref[:, slot, comp, :] = total[comp][slot][half:]


def local(slc, pairs, groups, tile_source):
    n_tile, n_pair = lax.axis_size("tile"), lax.axis_size("pair")
    e_dev, n_tiles, _, pixels = slc.shape
    tiles_dev = n_tiles // n_tile
    part = pixels // n_pair
    n_pairs = pairs.shape[0]
    n_epochs = e_dev * n_tile
    any_space = pl.BlockSpec(memory_space=pl.ANY)
    scalars = pl.BlockSpec(memory_space=pltpu.SMEM)
    vector = pl.BlockSpec(memory_space=pltpu.VMEM)
    ordered = pl.pallas_call(
        order_kernel,
        out_shape=jax.ShapeDtypeStruct((n_tile, e_dev, tiles_dev, 2, part), slc.dtype),
        in_specs=[scalars, any_space],
        out_specs=any_space,
        scratch_shapes=[pltpu.SemaphoreType.DMA],
        name="order",
    )(tile_source, slc)
    data = lax.all_to_all(ordered, "tile", split_axis=0, concat_axis=0, tiled=True)
    data = data.reshape(n_epochs, tiles_dev, 2, part // LANES, LANES)
    data = jnp.swapaxes(data, 2, 3).reshape(n_epochs, tiles_dev, 2 * part // LANES, LANES)
    pairs_t = pairs.T
    rows = n_pairs // 4 + n_epochs // n_pair
    parts = pl.pallas_call(
        terms_kernel,
        out_shape=jax.ShapeDtypeStruct((n_pair, rows, LANES), jnp.float32),
        in_specs=[scalars, vector, vector, vector],
        out_specs=vector,
        scratch_shapes=[
            pltpu.VMEM((8, tiles_dev, 32, LANES), jnp.float32),
            pltpu.VMEM((n_epochs, 2, tiles_dev, 16, LANES), jnp.float32),
            pltpu.VMEM((n_pairs, LANES), jnp.float32),
        ],
        compiler_params=pltpu.CompilerParams(vmem_limit_bytes=40 * 1024 * 1024),
        name="terms",
    )(pairs_t, data, pairs_t, groups.reshape(1, n_pairs))
    parts = lax.all_to_all(parts, "pair", split_axis=0, concat_axis=0, tiled=True)
    return pl.pallas_call(
        place_kernel,
        out_shape=(
            jax.ShapeDtypeStruct((n_epochs // n_pair, tiles_dev, 2, LANES), jnp.float32),
            jax.ShapeDtypeStruct((n_pairs // 2, tiles_dev, LANES), jnp.float32),
        ),
        in_specs=[vector],
        out_specs=(vector, vector),
        name="place",
    )(parts)


def solution(mesh):
    placed = (P("tile", None, None, None), P(), P(), P())
    return jax.shard_map(
        local,
        mesh=mesh,
        in_specs=placed,
        out_specs=(P("pair", "tile", None, None), P("pair", "tile", None)),
        check_vma=False,
    )
```

time: 520 us -> 173 us (0.33); the launches traced: 511 us -> 173 us
  waiting for transfers between devices: 201 us -> 0 us
  local copies, waits for them, and re-layouts: 161 us -> 0.01 us
  other arithmetic: 121 us -> 0 us
  Pallas kernels: 0 us -> 97.8 us
  blocking collectives: 0 us -> 74.3 us
  between operations: 14.5 us -> 0.66 us
  starting transfers between devices: 12.5 us -> 0 us
    all_to_all x1 -> x0, waiting for transfers between devices: 181 us -> none  [local(): lax.all_to_all(ordered, 'tile', split_axis=1, concat_axis=0, tiled=True)]
    pallas_call x0 -> x3, Pallas kernels: none -> 97.8 us  [the longest x1 65.3 us: local(): pl.pallas_call(order_kernel, out_shape=jax.ShapeDtypeStruct((n_tile, e_de...]
    gather x7 -> x0, local copies, waits for them, and re-layouts: 92.7 us -> none  [the longest x1 32.3 us: pair_terms(): ref_data = jnp.take(data, refs, axis=0)]
    all_to_all x0 -> x2, blocking collectives: none -> 74.3 us  [the longest x1 63.4 us: local(): lax.all_to_all(ordered, 'tile', split_axis=0, concat_axis=0, tiled=True)]
    select_n x6 -> x0, other arithmetic: 59.6 us -> none  [the longest x2 48.1 us: pair_terms(): sec_data = jnp.take(data, secs, axis=0)]
    slice x3 -> x0, local copies, waits for them, and re-layouts: 26.8 us -> none  [the longest x1 26.7 us: pair_terms(): d_re = data[:, :, 0].astype(jnp.float32)]
    add x2 -> x0, local copies, waits for them, and re-layouts: 23.6 us -> none  [the longest x1 14.7 us: pair_terms(): inter_re = box_means(a_re * b_re + a_im * b_im)]
    add x1 -> x0, other arithmetic: 22.8 us -> none  [pair_terms(): level = box_means(d_re * d_re + d_im * d_im)]
  transfers between devices with their start and end apart: 2 -> 0, of which waited for: 2 -> 0; matrix products, arithmetic and copies ran while one was open for 1% -> 0% of each run, Pallas kernels for 0% -> 0%
where the time goes in v1:
time: 173 us
  Pallas kernels  97.8 us (57%)
  blocking collectives  74.3 us (43%)
    pallas_call x1, Pallas kernels, local(): pl.pallas_call(order_kernel, out_shape=jax.ShapeDtypeStruct((n_tile, e_de...  65.3 us
    all_to_all x1, blocking collectives, local(): lax.all_to_all(ordered, 'tile', split_axis=0, concat_axis=0, tiled=True)  63.4 us
    pallas_call x1, Pallas kernels, local(): pl.pallas_call(terms_kernel, out_shape=jax.ShapeDtypeStruct((n_pair, rows...  30.2 us
    all_to_all x1, blocking collectives, local(): lax.all_to_all(parts, 'pair', split_axis=0, concat_axis=0, tiled=True)  10.9 us

profile of v1, /device:TPU:8, one launch (start us, length us, event | category | flops | bytes accessed | tf_op | source)
XLA Modules:
  0.0 172.7 jit_solution(9278037366136115764)
XLA Ops:
  0.6 65.3 %order.1 = bf16[64,2,2,2,2048]{4,3,2,1,0:T(2,128)(2,1)} custom-call(s32[128]{0:T(128)} %source_ref.1, bf16[2,128,2,8192]{3,2,1,0:T(2,128)(2,1)} %slc_ref.1), custom_call_target="tpu_custom_call" | custom-call | tf_op jit(solution)/shard_map/order/pallas_call | solution.py:180
  65.9 0.0 copy-start
  66.0 0.0 copy-start.1
  66.0 63.4 %all_to_all.10 = bf16[64,2,2,2,2048]{4,3,2,1,0:T(2,128)(2,1)S(1)} all-to-all(bf16[64,2,2,2,2048]{4,3,2,1,0:T(2,128)(2,1)} %order.1), channel_id=1, replica_groups=mesh['tile'=64,'pair'=4] {'tile'}, dimensions={0} | all-to-all | bytes 4194304 | tf_op jit(solution)/shard_map/all_to_all | solution.py:188
  129.3 0.0 copy-done
  129.4 0.0 copy-done.1
  129.4 30.2 %terms.1 = f32[4,128,128]{2,1,0:T(8,128)S(1)} custom-call(s32[2,384]{1,0:T(2,128)S(1)} %bitcast.8, bf16[128,2,32,128]{3,2,1,0:T(8,128)(2,1)S(1)} %bitcast.7, s32[2,384]{1,0:T(2,128)S(1)} %bitcast.9, s32[1,384]{1,0:T(1,128)S(1)} %bitcast.10), custom_call_target="tpu_custom_call" | custom-call | tf_op jit(solution)/shard_map/terms/pallas_call | solution.py:193
  159.6 10.9 %all_to_all.11.parts_ref = f32[4,128,128]{2,1,0:T(8,128)} all-to-all(f32[4,128,128]{2,1,0:T(8,128)S(1)} %terms.1), channel_id=1, replica_groups=mesh['tile'=64,'pair'=4] {'pair'}, dimensions={0} | all-to-all | bytes 524288 | tf_op jit(solution)/shard_map/all_to_all | solution.py:206
  170.4 2.3 %place.1 = (f32[32,2,2,128]{3,2,1,0:T(2,128)}, f32[192,2,128]{2,1,0:T(2,128)}) custom-call(f32[4,128,128]{2,1,0:T(8,128)} %all_to_all.11.parts_ref), custom_call_target="tpu_custom_call" | custom-call | tf_op jit(solution)/shard_map/place/pallas_call | solution.py:207
Async XLA Ops:
  65.9 63.4 %copy-start = (s32[384,2]{0,1:T(2,128)S(1)}, s32[384,2]{0,1:T(2,128)}, u32[]{:S(2)}) copy-start(s32[384,2]{0,1:T(2,128)} %param.5) | copy-start | bytes 9220
  66.0 63.4 %copy-start.1 = (s32[384,1]{0,1:T(1,128)S(1)}, s32[384,1]{0,1:T(1,128)}, u32[]{:S(2)}) copy-start(s32[384,1]{0,1:T(1,128)} %param.6) | copy-start | bytes 4612

commit v2 on v1

--- a/solution.py
+++ b/solution.py
@@ -63,7 +63,7 @@
     cols_i = lax.broadcasted_iota(jnp.int32, (LANES, LANES), 1)
     same_look = (rows_i // 16 == cols_i // 16).astype(jnp.bfloat16)
 
-    @pl.loop(0, n_epochs // step)
+    @pl.loop(0, n_epochs // step, unroll=2)
     def _(block):
         at = pl.ds(block * step, step)
         wide[...] = data_ref[at].astype(jnp.float32)
@@ -78,7 +78,7 @@
         norm[at, 0] = re * inv
         norm[at, 1] = im * inv
 
-    @pl.loop(0, n_pairs // BATCH)
+    @pl.loop(0, n_pairs // BATCH, unroll=8)
     def _(batch):
         def one(j):
             q = batch * BATCH + j
@@ -181,7 +181,7 @@
         order_kernel,
         out_shape=jax.ShapeDtypeStruct((n_tile, e_dev, tiles_dev, 2, part), slc.dtype),
         in_specs=[scalars, any_space],
-        out_specs=any_space,
+        out_specs=vector,
         scratch_shapes=[pltpu.SemaphoreType.DMA],
         name="order",
     )(tile_source, slc)

time: 173 us -> 90 us (0.52)
  Pallas kernels: 97.8 us -> 14.7 us
    pallas_call x1, Pallas kernels: 65.3 us -> 3.64 us  [local(): pl.pallas_call(order_kernel, out_shape=jax.ShapeDtypeStruct((n_tile, e_de...]
    pallas_call x1, Pallas kernels: 30.2 us -> 8.76 us  [local(): pl.pallas_call(terms_kernel, out_shape=jax.ShapeDtypeStruct((n_pair, rows...]
where the time goes in v2:
time: 90 us; the launch traced here: 89.6 us
  blocking collectives  74.3 us (83%)
  Pallas kernels  14.7 us (16%)
    all_to_all x1, blocking collectives, local(): lax.all_to_all(ordered, 'tile', split_axis=0, concat_axis=0, tiled=True)  63.4 us
    all_to_all x1, blocking collectives, local(): lax.all_to_all(parts, 'pair', split_axis=0, concat_axis=0, tiled=True)  10.9 us
    pallas_call x1, Pallas kernels, local(): pl.pallas_call(terms_kernel, out_shape=jax.ShapeDtypeStruct((n_pair, rows...  8.76 us
    pallas_call x1, Pallas kernels, local(): pl.pallas_call(order_kernel, out_shape=jax.ShapeDtypeStruct((n_tile, e_de...  3.64 us
    pallas_call x1, Pallas kernels, local(): pl.pallas_call(place_kernel, out_shape=(jax.ShapeDtypeStruct((n_epochs //...  2.3 us

profile of v2, /device:TPU:8, one launch (start us, length us, event | category | flops | bytes accessed | tf_op | source)
XLA Modules:
  0.0 89.6 jit_solution(6369074650693962571)
XLA Ops:
  0.6 3.6 %order.1 = bf16[64,2,2,2,2048]{4,3,2,1,0:T(2,128)(2,1)} custom-call(s32[128]{0:T(128)} %source_ref.1, bf16[2,128,2,8192]{3,2,1,0:T(2,128)(2,1)} %slc_ref.1), custom_call_target="tpu_custom_call" | custom-call | tf_op jit(solution)/shard_map/order/pallas_call | solution.py:180
  4.3 0.0 copy-start
  4.3 0.0 copy-start.1
  4.3 63.4 %all_to_all.10 = bf16[64,2,2,2,2048]{4,3,2,1,0:T(2,128)(2,1)S(1)} all-to-all(bf16[64,2,2,2,2048]{4,3,2,1,0:T(2,128)(2,1)} %order.1), channel_id=1, replica_groups=mesh['tile'=64,'pair'=4] {'tile'}, dimensions={0} | all-to-all | bytes 4194304 | tf_op jit(solution)/shard_map/all_to_all | solution.py:188
  67.7 0.0 copy-done
  67.7 0.0 copy-done.1
  67.7 8.8 %terms.1 = f32[4,128,128]{2,1,0:T(8,128)S(1)} custom-call(s32[2,384]{1,0:T(2,128)S(1)} %bitcast.8, bf16[128,2,32,128]{3,2,1,0:T(8,128)(2,1)S(1)} %bitcast.7, s32[2,384]{1,0:T(2,128)S(1)} %bitcast.9, s32[1,384]{1,0:T(1,128)S(1)} %bitcast.10), custom_call_target="tpu_custom_call" | custom-call | tf_op jit(solution)/shard_map/terms/pallas_call | solution.py:193
  76.4 10.9 %all_to_all.11.parts_ref = f32[4,128,128]{2,1,0:T(8,128)} all-to-all(f32[4,128,128]{2,1,0:T(8,128)S(1)} %terms.1), channel_id=1, replica_groups=mesh['tile'=64,'pair'=4] {'pair'}, dimensions={0} | all-to-all | bytes 524288 | tf_op jit(solution)/shard_map/all_to_all | solution.py:206
  87.3 2.3 %place.1 = (f32[32,2,2,128]{3,2,1,0:T(2,128)}, f32[192,2,128]{2,1,0:T(2,128)}) custom-call(f32[4,128,128]{2,1,0:T(8,128)} %all_to_all.11.parts_ref), custom_call_target="tpu_custom_call" | custom-call | tf_op jit(solution)/shard_map/place/pallas_call | solution.py:207
Async XLA Ops:
  4.3 63.4 %copy-start = (s32[384,2]{0,1:T(2,128)S(1)}, s32[384,2]{0,1:T(2,128)}, u32[]{:S(2)}) copy-start(s32[384,2]{0,1:T(2,128)} %param.5) | copy-start | bytes 9220
  4.3 63.4 %copy-start.1 = (s32[384,1]{0,1:T(1,128)S(1)}, s32[384,1]{0,1:T(1,128)}, u32[]{:S(2)}) copy-start(s32[384,1]{0,1:T(1,128)} %param.6) | copy-start | bytes 4612

commit v3 on v2

v3 whole, which is shorter than its diff:
```python
import functools

import jax
import jax.numpy as jnp
from jax import lax
from jax.experimental import pallas as pl
from jax.experimental.pallas import tpu as pltpu
from jax.sharding import PartitionSpec as P

EPS = 1e-06
LOOK_PIXELS = 64
LANES = 128
BATCH = 8


def split_dot(ones, x):
    high = x.astype(jnp.bfloat16)
    rest = x - high.astype(jnp.float32)
    middle = rest.astype(jnp.bfloat16)
    low = (rest - middle.astype(jnp.float32)).astype(jnp.bfloat16)
    width = x.shape[1]
    out = jnp.dot(ones, jnp.concatenate([high, middle, low], axis=1), preferred_element_type=jnp.float32)
    return out[:, :width] + out[:, width : 2 * width] + out[:, 2 * width :]


def dot_split(x, ones):
    high = x.astype(jnp.bfloat16)
    rest = x - high.astype(jnp.float32)
    middle = rest.astype(jnp.bfloat16)
    low = (rest - middle.astype(jnp.float32)).astype(jnp.bfloat16)
    rows = x.shape[0]
    out = jnp.dot(jnp.concatenate([high, middle, low], axis=0), ones, preferred_element_type=jnp.float32)
    return out[:rows] + out[rows : 2 * rows] + out[2 * rows :]


def order_kernel(source_ref, slc_ref, groups_ref, held, slot_ref, in_sem):
    n_dev, _, tiles_dev, _, part = held.shape
    n_chunks = in_sem.shape[0]
    chunk = n_dev // n_chunks
    start = pl.multiple_of(lax.axis_index("pair") * part, part)

    for c in range(n_chunks):

        @pl.loop(c * chunk, (c + 1) * chunk, unroll=4)
        def _(d):
            for k in range(tiles_dev):
                src = source_ref[d * tiles_dev + k]
                pltpu.make_async_copy(
                    slc_ref.at[:, src, :, pl.ds(start, part)], held.at[d, :, k], in_sem.at[c]
                ).start()

    groups = groups_ref[0:1, :]
    n_pairs = groups.shape[1]
    mine = (lax.broadcasted_iota(jnp.int32, (8, n_pairs), 0) == groups).astype(jnp.float32)
    before = (
        lax.broadcasted_iota(jnp.int32, (n_pairs, n_pairs), 0)
        < lax.broadcasted_iota(jnp.int32, (n_pairs, n_pairs), 1)
    )
    ranks = jnp.dot(
        mine.astype(jnp.bfloat16), before.astype(jnp.bfloat16), preferred_element_type=jnp.float32
    )
    rank = jnp.sum(mine * ranks, axis=0, keepdims=True).astype(jnp.int32)
    half = n_pairs // 4
    slot = jnp.where(rank < half, groups * half + rank, n_pairs + groups * half + rank - half)
    slot_ref[...] = jnp.broadcast_to(slot, slot_ref.shape)

    for c in range(n_chunks):
        at = pl.ds(c * chunk, chunk)
        pltpu.make_async_copy(held.at[at], held.at[at], in_sem.at[c]).wait()


def terms_kernel(pairs_sm, data_ref, pairs_ref, slot_ref, *refs):
    out_refs, (wide, norm, gamma, chosen_ref, rhs_ref) = refs[:-5], refs[-5:]
    n_epochs = data_ref.shape[0]
    n_pairs = pairs_ref.shape[1]
    step = wide.shape[0]
    sub = lax.broadcasted_iota(jnp.int32, (8, LANES), 0)
    lane = lax.broadcasted_iota(jnp.int32, (8, LANES), 1)
    first = sub < 4
    rows_i = lax.broadcasted_iota(jnp.int32, (LANES, LANES), 0)
    cols_i = lax.broadcasted_iota(jnp.int32, (LANES, LANES), 1)
    same_look = (rows_i // 16 == cols_i // 16).astype(jnp.bfloat16)

    @pl.loop(0, n_epochs // step, unroll=4)
    def _(block):
        at = pl.ds(block * step, step)
        wide[...] = data_ref[at].astype(jnp.float32)
        re = wide[:, :, pl.ds(0, 16, stride=2), :]
        im = wide[:, :, pl.ds(1, 16, stride=2), :]
        power = re * re + im * im
        lines = power[:, :, 0:8] + power[:, :, 8:16]
        lines = lines + pltpu.roll(lines, 4, 2)
        level = dot_split(lines.reshape(step * 2 * 8, LANES), same_look).reshape(step, 2, 8, LANES)
        inv = lax.rsqrt(level * (1.0 / LOOK_PIXELS) + EPS) * 0.125
        inv = jnp.concatenate([inv, inv], axis=2)
        norm[at, 0] = re * inv
        norm[at, 1] = im * inv

    @pl.loop(0, n_pairs // BATCH, unroll=8)
    def _(batch):
        def one(j):
            q = batch * BATCH + j
            r = pairs_sm[0, q]
            t = pairs_sm[1, q]
            a_re, a_im = norm[r, 0], norm[r, 1]
            b_re, b_im = norm[t, 0], norm[t, 1]
            parts = []
            for cross in (a_re * b_re + a_im * b_im, a_im * b_re - a_re * b_im):
                s0 = cross[0, 0:8] + cross[0, 8:16]
                s1 = cross[1, 0:8] + cross[1, 8:16]
                parts.append(jnp.where(first, s0, s1) + pltpu.roll(jnp.where(first, s1, s0), 4, 0))
            return merge(parts[0], parts[1], 8)

        def merge(a, b, k):
            return jnp.where(
                (lane & k) == 0, a + pltpu.roll(a, LANES - k, 1), b + pltpu.roll(b, k, 1)
            )

        def tree(js, k):
            if len(js) == 1:
                return one(js[0])
            return merge(tree([j for j in js if not j & k], k // 2), tree([j for j in js if j & k], k // 2), k)

        z = tree(list(range(BATCH)), 4)
        gamma[batch] = z

    z = gamma[...]
    sub = lax.broadcasted_iota(jnp.int32, z.shape, 1)
    lane = lax.broadcasted_iota(jnp.int32, z.shape, 2)
    for k in (4, 2, 1):
        up = pltpu.roll(pltpu.roll(z, k, 2), 8 - k, 1)
        down = pltpu.roll(pltpu.roll(z, LANES - k, 2), k, 1)
        low_row, low_lane = (sub & k) == 0, (lane & k) == 0
        z = jnp.where(low_row == low_lane, z, jnp.where(low_row, up, down))
    z = z.reshape(n_pairs, LANES)
    comp0 = (lax.broadcasted_iota(jnp.int32, z.shape, 1) & 8) == 0
    square = z * z
    weight = square + jnp.where(comp0, pltpu.roll(square, LANES - 8, 1), pltpu.roll(square, 8, 1))
    refs, secs = pairs_ref[0:1, :], pairs_ref[1:2, :]
    epochs = lax.broadcasted_iota(jnp.int32, (n_epochs, n_pairs), 0)
    incidence = (epochs == secs).astype(jnp.float32) - (epochs == refs).astype(jnp.float32)
    rhs_ref[...] = split_dot(incidence.astype(jnp.bfloat16), weight * z)
    slot = slot_ref[0:1, :]
    hit = (lax.broadcasted_iota(jnp.int32, (2 * n_pairs, n_pairs), 0) == slot).astype(jnp.bfloat16)
    chosen = split_dot(hit, weight)
    chosen_ref[...] = jnp.where(comp0, chosen[:n_pairs], chosen[n_pairs:])
    n_members = len(out_refs)
    half, e_out = n_pairs // n_members, n_epochs // n_members
    me = lax.axis_index("pair")
    for k, out_ref in enumerate(out_refs):
        to = lax.rem(me + k, n_members)
        out_ref[0:half, :] = chosen_ref[pl.ds(pl.multiple_of(to * half, half), half), :]
        out_ref[half : half + e_out, :] = rhs_ref[pl.ds(pl.multiple_of(to * e_out, e_out), e_out), :]


def place_kernel(*refs):
    part_refs, (rhs_ref, coherence_ref) = refs[:-2], refs[-2:]
    n_members = len(part_refs)
    rows = part_refs[0].shape[0]
    half = coherence_ref.shape[0] // 2
    width = LANES // n_members
    me = lax.axis_index("pair")
    i = lax.broadcasted_iota(jnp.int32, (LANES, LANES), 0)
    j = lax.broadcasted_iota(jnp.int32, (LANES, LANES), 1)
    ones = (j == (i % 16) * 8 + i // 16).astype(jnp.bfloat16)
    parts = dot_split(jnp.concatenate([r[...] for r in part_refs], axis=0), ones)
    owner = lax.broadcasted_iota(jnp.int32, (rows, LANES), 1) // width
    total = [None] * 4
    for k in range(n_members):
        member = lax.rem(me + n_members - k, n_members)
        own = owner == member
        base = pltpu.roll(parts[k * rows : (k + 1) * rows], member * width, 1)
        for g in range(4):
            piece = base if g == 0 else pltpu.roll(base, LANES - g * width, 1)
            total[g] = piece if k == 0 else jnp.where(own, piece, total[g])
    for comp in range(2):
        for slot in range(2):
            coherence_ref[pl.ds(comp * half, half), slot, :] = total[comp * 2 + slot][:half]
            rhs_ref[:, slot, comp, :] = total[comp * 2 + slot][half:]


def local(slc, pairs, groups, tile_source):
    n_tile, n_pair = lax.axis_size("tile"), lax.axis_size("pair")
    e_dev, n_tiles, _, pixels = slc.shape
    tiles_dev = n_tiles // n_tile
    part = pixels // n_pair
    n_pairs = pairs.shape[0]
    n_epochs = e_dev * n_tile
    in_hbm = pl.BlockSpec(memory_space=pltpu.HBM)
    scalars = pl.BlockSpec(memory_space=pltpu.SMEM)
    vector = pl.BlockSpec(memory_space=pltpu.VMEM)
    pairs_t, groups_t = pairs.T, groups.reshape(1, n_pairs)
    out_shape = (n_tile, e_dev, tiles_dev, 2, part)
    chunks = 4
    ordered, slots = pl.pallas_call(
        order_kernel,
        out_shape=(
            jax.ShapeDtypeStruct(out_shape, slc.dtype),
            jax.ShapeDtypeStruct((8, n_pairs), jnp.int32),
        ),
        in_specs=[scalars, in_hbm, vector],
        out_specs=(vector, vector),
        scratch_shapes=[
            pltpu.SemaphoreType.DMA((chunks,)),
        ],
        compiler_params=pltpu.CompilerParams(vmem_limit_bytes=8 * 1024 * 1024),
        name="order",
    )(tile_source, slc, groups_t)
    data = lax.all_to_all(ordered, "tile", split_axis=0, concat_axis=0, tiled=True)
    data = data.reshape(n_epochs, tiles_dev, 2, part // LANES, LANES)
    data = jnp.swapaxes(data, 2, 3).reshape(n_epochs, tiles_dev, 2 * part // LANES, LANES)
    rows = n_pairs // 4 + n_epochs // n_pair
    parts = pl.pallas_call(
        terms_kernel,
        out_shape=[jax.ShapeDtypeStruct((rows, LANES), jnp.float32)] * n_pair,
        in_specs=[scalars, vector, vector, vector],
        out_specs=[vector] * n_pair,
        scratch_shapes=[
            pltpu.VMEM((8, tiles_dev, 32, LANES), jnp.float32),
            pltpu.VMEM((n_epochs, 2, tiles_dev, 16, LANES), jnp.float32),
            pltpu.VMEM((n_pairs // BATCH, BATCH, LANES), jnp.float32),
            pltpu.VMEM((n_pairs, LANES), jnp.float32),
            pltpu.VMEM((n_epochs, LANES), jnp.float32),
        ],
        compiler_params=pltpu.CompilerParams(vmem_limit_bytes=40 * 1024 * 1024),
        name="terms",
    )(pairs_t, data, pairs_t, slots)
    parts = [
        part_k if k == 0 else lax.ppermute(part_k, "pair", [(i, (i + k) % n_pair) for i in range(n_pair)])
        for k, part_k in enumerate(parts)
    ]
    return pl.pallas_call(
        place_kernel,
        out_shape=(
            jax.ShapeDtypeStruct((n_epochs // n_pair, tiles_dev, 2, LANES), jnp.float32),
            jax.ShapeDtypeStruct((n_pairs // 2, tiles_dev, LANES), jnp.float32),
        ),
        in_specs=[vector] * n_pair,
        out_specs=(vector, vector),
        compiler_params=pltpu.CompilerParams(vmem_limit_bytes=8 * 1024 * 1024),
        name="place",
    )(*parts)


def solution(mesh):
    placed = (P("tile", None, None, None), P(), P(), P())
    return jax.shard_map(
        local,
        mesh=mesh,
        in_specs=placed,
        out_specs=(P("pair", "tile", None, None), P("pair", "tile", None)),
        check_vma=False,
    )
```

time: 90 us -> 88.9 us (0.988)
  blocking collectives: 74.3 us -> 63.2 us
  starting transfers between devices: 0 us -> 5.74 us
  local copies, waits for them, and re-layouts: 0.01 us -> 4.72 us
  Pallas kernels: 14.7 us -> 11.6 us
  waiting for transfers between devices: 0 us -> 2.82 us
    all_to_all x1 -> x0, blocking collectives: 10.9 us -> none  [local(): lax.all_to_all(parts, 'pair', split_axis=0, concat_axis=0, tiled=True)]
    ppermute x0 -> x3, starting transfers between devices: none -> 5.74 us  [local(): lax.ppermute(part_k, 'pair', [(i, (i + k) % n_pair) for i in range(n_pair)])]
    unnamed x4 -> x8, local copies, waits for them, and re-layouts: 0.01 us -> 4.72 us
    ppermute x0 -> x3, waiting for transfers between devices: none -> 2.82 us  [local(): lax.ppermute(part_k, 'pair', [(i, (i + k) % n_pair) for i in range(n_pair)])]
    pallas_call x2, Pallas kernels: 12.4 us -> 10.3 us  [the longest x1 7.5 us: local(): pl.pallas_call(terms_kernel, out_shape=[jax.ShapeDtypeStruct((rows, LANES...]
    pallas_call x1, Pallas kernels: 2.3 us -> 1.26 us  [local(): pl.pallas_call(place_kernel, out_shape=(jax.ShapeDtypeStruct((n_epochs //...]
  transfers between devices with their start and end apart: 0 -> 3, of which waited for: 0 -> 2; matrix products, arithmetic and copies ran while one was open for 0% -> 0% of each run, Pallas kernels for 0% -> 0%
where the time goes in v3:
time: 88.9 us; the launch traced here: 88.7 us
  blocking collectives  63.2 us (71%)
  Pallas kernels  11.6 us (13%)
  starting transfers between devices  5.74 us (6%)
  local copies, waits for them, and re-layouts  4.72 us (5%)
  waiting for transfers between devices  2.82 us (3%)
    all_to_all x1, blocking collectives, local(): lax.all_to_all(ordered, 'tile', split_axis=0, concat_axis=0, tiled=True)  63.2 us
    pallas_call x1, Pallas kernels, local(): pl.pallas_call(terms_kernel, out_shape=[jax.ShapeDtypeStruct((rows, LANES...  7.5 us
    ppermute x3, starting transfers between devices, local(): lax.ppermute(part_k, 'pair', [(i, (i + k) % n_pair) for i in range(n_pair)])  5.74 us
    unnamed x8, local copies, waits for them, and re-layouts  4.72 us
    ppermute x3, waiting for transfers between devices, local(): lax.ppermute(part_k, 'pair', [(i, (i + k) % n_pair) for i in range(n_pair)])  2.82 us
    pallas_call x1, Pallas kernels, local(): pl.pallas_call(order_kernel, out_shape=(jax.ShapeDtypeStruct(out_shape, s...  2.82 us
  transfers between devices with their start and end apart: 3, of which 2 were waited for; matrix products, arithmetic and copies ran while one was open for 0% of the time, Pallas kernels for 0%

profile of v3, /device:TPU:8, one launch (start us, length us, event | category | flops | bytes accessed | tf_op | source)
XLA Modules:
  0.0 88.7 jit_solution(12753736981704422558)
XLA Ops:
  0.6 0.0 copy-start
  0.6 3.4 %copy-done = bf16[2,128,2,8192]{3,2,1,0:T(2,128)(2,1)S(1)} copy-done((bf16[2,128,2,8192]{3,2,1,0:T(2,128)(2,1)S(1)}, bf16[2,128,2,8192]{3,2,1,0:T(2,128)(2,1)}, u32[]{:S(2)}) %copy-start) | copy-done | bytes 8388632
  4.0 0.0 copy-start.2
  4.0 0.7 copy-done.2
  4.7 0.0 copy-start.3
  4.7 0.7 copy-done.3
  5.3 2.8 %order.1 = (bf16[64,2,2,2,2048]{4,3,2,1,0:T(2,128)(2,1)S(1)}, s32[8,384]{1,0:T(8,128)S(1)}) custom-call(s32[128]{0:T(128)S(1)} %copy-done.3, bf16[2,128,2,8192]{3,2,1,0:T(2,128)(2,1)S(1)} %copy-done, s32[1,384]{1,0:T(1,128)S(1)} %bitcast.10), custom_call_target="tpu_custom_call" | custom-call | tf_op jit(solution)/shard_map/order/pallas_call | solution.py:195
  8.2 0.0 copy-start.1
  8.2 63.2 %all_to_all.5 = bf16[64,2,2,2,2048]{4,3,2,1,0:T(2,128)(2,1)S(1)} all-to-all(bf16[64,2,2,2,2048]{4,3,2,1,0:T(2,128)(2,1)S(1)} %get-tuple-element.8), channel_id=1, replica_groups=mesh['tile'=64,'pair'=4] {'tile'}, dimensions={0} | all-to-all | bytes 4194304 | tf_op jit(solution)/shard_map/all_to_all | solution.py:209
  71.3 0.0 copy-done.1
  71.4 7.5 %terms.1 = (f32[128,128]{1,0:T(8,128)S(1)}, f32[128,128]{1,0:T(8,128)S(1)}, f32[128,128]{1,0:T(8,128)S(1)}, f32[128,128]{1,0:T(8,128)S(1)}) custom-call(s32[2,384]{1,0:T(2,128)S(1)} %bitcast.8, bf16[128,2,32,128]{3,2,1,0:T(8,128)(2,1)S(1)} %bitcast.7, s32[2,384]{1,0:T(2,128)S(1)} %bitcast.9, s32[8,384]{1,0:T(8,128)S(1)} %get-tuple-element.9.slot_ref), custom_call_target="tpu_custom_call" | custom-call | tf_op jit(solution)/shard_map/terms/pallas_call | solution.py:213
  78.9 1.6 %collective-permute-start = (f32[128,128]{1,0:T(8,128)S(1)}, f32[128,128]{1,0:T(8,128)S(1)}, u32[]{:S(2)}, u32[]{:S(2)}) collective-permute-start(f32[128,128]{1,0:T(8,128)S(1)} %get-tuple-element.11), channel_id=1, source_target_pairs={{0,1},{1,2},{2,3},{3,0},{4,5},{5,6},{6,7},{7,4},{8,9},{9,10},{10,1... | collective-permute-start | bytes 196616 | tf_op jit(solution)/shard_map/ppermute | solution.py:229
  80.4 2.7 %collective-permute-start.1 = (f32[128,128]{1,0:T(8,128)S(1)}, f32[128,128]{1,0:T(8,128)S(1)}, u32[]{:S(2)}, u32[]{:S(2)}) collective-permute-start(f32[128,128]{1,0:T(8,128)S(1)} %get-tuple-element.12), channel_id=1, source_target_pairs={{0,2},{1,3},{2,0},{3,1},{4,6},{5,7},{6,4},{7,5},{8,10},{9,11},{10,... | collective-permute-start | bytes 196616 | tf_op jit(solution)/shard_map/ppermute | solution.py:229
  83.2 1.4 %collective-permute-start.2 = (f32[128,128]{1,0:T(8,128)S(1)}, f32[128,128]{1,0:T(8,128)S(1)}, u32[]{:S(2)}, u32[]{:S(2)}) collective-permute-start(f32[128,128]{1,0:T(8,128)S(1)} %get-tuple-element.13), channel_id=1, source_target_pairs={{0,3},{1,0},{2,1},{3,2},{4,7},{5,4},{6,5},{7,6},{8,11},{9,8},{10,9... | collective-permute-start | bytes 196616 | tf_op jit(solution)/shard_map/ppermute | solution.py:229
  84.6 0.0 collective-permute-done.refs_1_
  84.6 1.6 %collective-permute-done.1.refs_2_ = f32[128,128]{1,0:T(8,128)S(1)} collective-permute-done((f32[128,128]{1,0:T(8,128)S(1)}, f32[128,128]{1,0:T(8,128)S(1)}, u32[]{:S(2)}, u32[]{:S(2)}) %collective-permute-start.1) | collective-permute-done | bytes 65568 | tf_op jit(solution)/shard_map/ppermute | solution.py:229
  86.2 1.2 %collective-permute-done.2.refs_3_ = f32[128,128]{1,0:T(8,128)S(1)} collective-permute-done((f32[128,128]{1,0:T(8,128)S(1)}, f32[128,128]{1,0:T(8,128)S(1)}, u32[]{:S(2)}, u32[]{:S(2)}) %collective-permute-start.2) | collective-permute-done | bytes 65568 | tf_op jit(solution)/shard_map/ppermute | solution.py:229
  87.4 1.3 %place.1 = (f32[32,2,2,128]{3,2,1,0:T(2,128)}, f32[192,2,128]{2,1,0:T(2,128)}) custom-call(f32[128,128]{1,0:T(8,128)S(1)} %get-tuple-element.10.refs_0_, f32[128,128]{1,0:T(8,128)S(1)} %collective-permute-done.refs_1_, f32[128,128]{1,0:T(8,128)S(1)} %collective-permute-done.1.refs_2_, f32[128,128]{1,0:T(8,128)S(1)} %collective-permute-done.2.refs_3_), custom_call_target="tpu_custom_call" | custom-call | tf_op jit(solution)/shard_map/place/pallas_call | solution.py:232
Async XLA Ops:
  0.6 3.4 %copy-start = (bf16[2,128,2,8192]{3,2,1,0:T(2,128)(2,1)S(1)}, bf16[2,128,2,8192]{3,2,1,0:T(2,128)(2,1)}, u32[]{:S(2)}) copy-start(bf16[2,128,2,8192]{3,2,1,0:T(2,128)(2,1)} %slc_ref.1) | copy-start | bytes 25165828
  4.0 0.7 copy-start.2
  4.7 0.7 copy-start.3
  8.2 63.2 %copy-start.1 = (s32[384,2]{0,1:T(2,128)S(1)}, s32[384,2]{0,1:T(2,128)}, u32[]{:S(2)}) copy-start(s32[384,2]{0,1:T(2,128)} %param.5) | copy-start | bytes 9220
  78.9 5.7 %collective-permute-start = (f32[128,128]{1,0:T(8,128)S(1)}, f32[128,128]{1,0:T(8,128)S(1)}, u32[]{:S(2)}, u32[]{:S(2)}) collective-permute-start(f32[128,128]{1,0:T(8,128)S(1)} %get-tuple-element.11), channel_id=1, source_target_pairs={{0,1},{1,2},{2,3},{3,0},{4,5},{5,6},{6,7},{7,4},{8,9},{9,10},{10,1... | collective-permute-start | bytes 196616 | tf_op jit(solution)/shard_map/ppermute | solution.py:229
  80.4 5.8 %collective-permute-start.1 = (f32[128,128]{1,0:T(8,128)S(1)}, f32[128,128]{1,0:T(8,128)S(1)}, u32[]{:S(2)}, u32[]{:S(2)}) collective-permute-start(f32[128,128]{1,0:T(8,128)S(1)} %get-tuple-element.12), channel_id=1, source_target_pairs={{0,2},{1,3},{2,0},{3,1},{4,6},{5,7},{6,4},{7,5},{8,10},{9,11},{10,... | collective-permute-start | bytes 196616 | tf_op jit(solution)/shard_map/ppermute | solution.py:229
  83.2 4.3 %collective-permute-start.2 = (f32[128,128]{1,0:T(8,128)S(1)}, f32[128,128]{1,0:T(8,128)S(1)}, u32[]{:S(2)}, u32[]{:S(2)}) collective-permute-start(f32[128,128]{1,0:T(8,128)S(1)} %get-tuple-element.13), channel_id=1, source_target_pairs={{0,3},{1,0},{2,1},{3,2},{4,7},{5,4},{6,5},{7,6},{8,11},{9,8},{10,9... | collective-permute-start | bytes 196616 | tf_op jit(solution)/shard_map/ppermute | solution.py:229

commit v4 on v3

--- a/solution.py
+++ b/solution.py
@@ -33,7 +33,7 @@
     return out[:rows] + out[rows : 2 * rows] + out[2 * rows :]
 
 
-def order_kernel(source_ref, slc_ref, groups_ref, held, slot_ref, in_sem):
+def order_kernel(source_ref, slc_ref, held, in_sem):
     n_dev, _, tiles_dev, _, part = held.shape
     n_chunks = in_sem.shape[0]
     chunk = n_dev // n_chunks
@@ -49,27 +49,12 @@
                     slc_ref.at[:, src, :, pl.ds(start, part)], held.at[d, :, k], in_sem.at[c]
                 ).start()
 
-    groups = groups_ref[0:1, :]
-    n_pairs = groups.shape[1]
-    mine = (lax.broadcasted_iota(jnp.int32, (8, n_pairs), 0) == groups).astype(jnp.float32)
-    before = (
-        lax.broadcasted_iota(jnp.int32, (n_pairs, n_pairs), 0)
-        < lax.broadcasted_iota(jnp.int32, (n_pairs, n_pairs), 1)
-    )
-    ranks = jnp.dot(
-        mine.astype(jnp.bfloat16), before.astype(jnp.bfloat16), preferred_element_type=jnp.float32
-    )
-    rank = jnp.sum(mine * ranks, axis=0, keepdims=True).astype(jnp.int32)
-    half = n_pairs // 4
-    slot = jnp.where(rank < half, groups * half + rank, n_pairs + groups * half + rank - half)
-    slot_ref[...] = jnp.broadcast_to(slot, slot_ref.shape)
-
     for c in range(n_chunks):
         at = pl.ds(c * chunk, chunk)
         pltpu.make_async_copy(held.at[at], held.at[at], in_sem.at[c]).wait()
 
 
-def terms_kernel(pairs_sm, data_ref, pairs_ref, slot_ref, *refs):
+def terms_kernel(pairs_sm, data_ref, pairs_ref, groups_ref, *refs):
     out_refs, (wide, norm, gamma, chosen_ref, rhs_ref) = refs[:-5], refs[-5:]
     n_epochs = data_ref.shape[0]
     n_pairs = pairs_ref.shape[1]
@@ -140,7 +125,18 @@
     epochs = lax.broadcasted_iota(jnp.int32, (n_epochs, n_pairs), 0)
     incidence = (epochs == secs).astype(jnp.float32) - (epochs == refs).astype(jnp.float32)
     rhs_ref[...] = split_dot(incidence.astype(jnp.bfloat16), weight * z)
-    slot = slot_ref[0:1, :]
+    groups = groups_ref[0:1, :]
+    mine = (lax.broadcasted_iota(jnp.int32, (8, n_pairs), 0) == groups).astype(jnp.float32)
+    before = (
+        lax.broadcasted_iota(jnp.int32, (n_pairs, n_pairs), 0)
+        < lax.broadcasted_iota(jnp.int32, (n_pairs, n_pairs), 1)
+    )
+    ranks = jnp.dot(
+        mine.astype(jnp.bfloat16), before.astype(jnp.bfloat16), preferred_element_type=jnp.float32
+    )
+    rank = jnp.sum(mine * ranks, axis=0, keepdims=True).astype(jnp.int32)
+    half = n_pairs // 4
+    slot = jnp.where(rank < half, groups * half + rank, n_pairs + groups * half + rank - half)
     hit = (lax.broadcasted_iota(jnp.int32, (2 * n_pairs, n_pairs), 0) == slot).astype(jnp.bfloat16)
     chosen = split_dot(hit, weight)
     chosen_ref[...] = jnp.where(comp0, chosen[:n_pairs], chosen[n_pairs:])
@@ -192,20 +188,17 @@
     pairs_t, groups_t = pairs.T, groups.reshape(1, n_pairs)
     out_shape = (n_tile, e_dev, tiles_dev, 2, part)
     chunks = 4
-    ordered, slots = pl.pallas_call(
+    ordered = pl.pallas_call(
         order_kernel,
-        out_shape=(
-            jax.ShapeDtypeStruct(out_shape, slc.dtype),
-            jax.ShapeDtypeStruct((8, n_pairs), jnp.int32),
-        ),
-        in_specs=[scalars, in_hbm, vector],
-        out_specs=(vector, vector),
+        out_shape=jax.ShapeDtypeStruct(out_shape, slc.dtype),
+        in_specs=[scalars, in_hbm],
+        out_specs=vector,
         scratch_shapes=[
             pltpu.SemaphoreType.DMA((chunks,)),
         ],
-        compiler_params=pltpu.CompilerParams(vmem_limit_bytes=8 * 1024 * 1024),
+        compiler_params=pltpu.CompilerParams(vmem_limit_bytes=48 * 1024 * 1024),
         name="order",
-    )(tile_source, slc, groups_t)
+    )(tile_source, slc)
     data = lax.all_to_all(ordered, "tile", split_axis=0, concat_axis=0, tiled=True)
     data = data.reshape(n_epochs, tiles_dev, 2, part // LANES, LANES)
     data = jnp.swapaxes(data, 2, 3).reshape(n_epochs, tiles_dev, 2 * part // LANES, LANES)
@@ -224,7 +217,7 @@
         ],
         compiler_params=pltpu.CompilerParams(vmem_limit_bytes=40 * 1024 * 1024),
         name="terms",
-    )(pairs_t, data, pairs_t, slots)
+    )(pairs_t, data, pairs_t, groups_t)
     parts = [
         part_k if k == 0 else lax.ppermute(part_k, "pair", [(i, (i + k) % n_pair) for i in range(n_pair)])
         for k, part_k in enumerate(parts)

time: 88.9 us -> 84.4 us (0.949)
  local copies, waits for them, and re-layouts: 4.72 us -> 0.66 us
    unnamed x8 -> x6, local copies, waits for them, and re-layouts: 4.72 us -> 0.66 us
where the time goes in v4:
time: 84.4 us; the launch traced here: 84.2 us
  blocking collectives  63.2 us (75%)
  Pallas kernels  11.1 us (13%)
  starting transfers between devices  5.73 us (7%)
  waiting for transfers between devices  2.83 us (3%)
    all_to_all x1, blocking collectives, local(): lax.all_to_all(ordered, 'tile', split_axis=0, concat_axis=0, tiled=True)  63.2 us
    pallas_call x1, Pallas kernels, local(): pl.pallas_call(terms_kernel, out_shape=[jax.ShapeDtypeStruct((rows, LANES...  7.67 us
    ppermute x3, starting transfers between devices, local(): lax.ppermute(part_k, 'pair', [(i, (i + k) % n_pair) for i in range(n_pair)])  5.73 us
    ppermute x3, waiting for transfers between devices, local(): lax.ppermute(part_k, 'pair', [(i, (i + k) % n_pair) for i in range(n_pair)])  2.83 us
    pallas_call x1, Pallas kernels, local(): pl.pallas_call(order_kernel, out_shape=jax.ShapeDtypeStruct(out_shape, sl...  2.19 us
  transfers between devices with their start and end apart: 3, of which 2 were waited for; matrix products, arithmetic and copies ran while one was open for 0% of the time, Pallas kernels for 0%

profile of v4, /device:TPU:8, one launch (start us, length us, event | category | flops | bytes accessed | tf_op | source)
XLA Modules:
  0.0 84.2 jit_solution(7088561021642044828)
XLA Ops:
  0.6 0.0 copy-start.2
  0.6 0.6 copy-done.2
  1.3 2.2 %order.1 = bf16[64,2,2,2,2048]{4,3,2,1,0:T(2,128)(2,1)S(1)} custom-call(s32[128]{0:T(128)S(1)} %copy-done.2, bf16[2,128,2,8192]{3,2,1,0:T(2,128)(2,1)} %slc_ref.1), custom_call_target="tpu_custom_call" | custom-call | tf_op jit(solution)/shard_map/order/pallas_call | solution.py:191
  3.5 0.0 copy-start
  3.5 0.0 copy-start.1
  3.5 63.2 %all_to_all.5 = bf16[64,2,2,2,2048]{4,3,2,1,0:T(2,128)(2,1)S(1)} all-to-all(bf16[64,2,2,2,2048]{4,3,2,1,0:T(2,128)(2,1)S(1)} %order.1), channel_id=1, replica_groups=mesh['tile'=64,'pair'=4] {'tile'}, dimensions={0} | all-to-all | bytes 4194304 | tf_op jit(solution)/shard_map/all_to_all | solution.py:202
  66.7 0.0 copy-done
  66.7 0.0 copy-done.1
  66.7 7.7 %terms.1 = (f32[128,128]{1,0:T(8,128)S(1)}, f32[128,128]{1,0:T(8,128)S(1)}, f32[128,128]{1,0:T(8,128)S(1)}, f32[128,128]{1,0:T(8,128)S(1)}) custom-call(s32[2,384]{1,0:T(2,128)S(1)} %bitcast.8, bf16[128,2,32,128]{3,2,1,0:T(8,128)(2,1)S(1)} %bitcast.7, s32[2,384]{1,0:T(2,128)S(1)} %bitcast.9, s32[1,384]{1,0:T(1,128)S(1)} %bitcast.10), custom_call_target="tpu_custom_call" | custom-call | tf_op jit(solution)/shard_map/terms/pallas_call | solution.py:206
  74.4 1.6 %collective-permute-start = (f32[128,128]{1,0:T(8,128)S(1)}, f32[128,128]{1,0:T(8,128)S(1)}, u32[]{:S(2)}, u32[]{:S(2)}) collective-permute-start(f32[128,128]{1,0:T(8,128)S(1)} %get-tuple-element.7), channel_id=1, source_target_pairs={{0,1},{1,2},{2,3},{3,0},{4,5},{5,6},{6,7},{7,4},{8,9},{9,10},{10,1... | collective-permute-start | bytes 196616 | tf_op jit(solution)/shard_map/ppermute | solution.py:222
  75.9 2.7 %collective-permute-start.1 = (f32[128,128]{1,0:T(8,128)S(1)}, f32[128,128]{1,0:T(8,128)S(1)}, u32[]{:S(2)}, u32[]{:S(2)}) collective-permute-start(f32[128,128]{1,0:T(8,128)S(1)} %get-tuple-element.8), channel_id=1, source_target_pairs={{0,2},{1,3},{2,0},{3,1},{4,6},{5,7},{6,4},{7,5},{8,10},{9,11},{10,... | collective-permute-start | bytes 196616 | tf_op jit(solution)/shard_map/ppermute | solution.py:222
  78.7 1.4 %collective-permute-start.2 = (f32[128,128]{1,0:T(8,128)S(1)}, f32[128,128]{1,0:T(8,128)S(1)}, u32[]{:S(2)}, u32[]{:S(2)}) collective-permute-start(f32[128,128]{1,0:T(8,128)S(1)} %get-tuple-element.9), channel_id=1, source_target_pairs={{0,3},{1,0},{2,1},{3,2},{4,7},{5,4},{6,5},{7,6},{8,11},{9,8},{10,9... | collective-permute-start | bytes 196616 | tf_op jit(solution)/shard_map/ppermute | solution.py:222
  80.1 0.0 collective-permute-done.refs_1_
  80.1 1.6 %collective-permute-done.1.refs_2_ = f32[128,128]{1,0:T(8,128)S(1)} collective-permute-done((f32[128,128]{1,0:T(8,128)S(1)}, f32[128,128]{1,0:T(8,128)S(1)}, u32[]{:S(2)}, u32[]{:S(2)}) %collective-permute-start.1) | collective-permute-done | bytes 65568 | tf_op jit(solution)/shard_map/ppermute | solution.py:222
  81.7 1.2 %collective-permute-done.2.refs_3_ = f32[128,128]{1,0:T(8,128)S(1)} collective-permute-done((f32[128,128]{1,0:T(8,128)S(1)}, f32[128,128]{1,0:T(8,128)S(1)}, u32[]{:S(2)}, u32[]{:S(2)}) %collective-permute-start.2) | collective-permute-done | bytes 65568 | tf_op jit(solution)/shard_map/ppermute | solution.py:222
  82.9 1.3 %place.1 = (f32[32,2,2,128]{3,2,1,0:T(2,128)}, f32[192,2,128]{2,1,0:T(2,128)}) custom-call(f32[128,128]{1,0:T(8,128)S(1)} %get-tuple-element.6.refs_0_, f32[128,128]{1,0:T(8,128)S(1)} %collective-permute-done.refs_1_, f32[128,128]{1,0:T(8,128)S(1)} %collective-permute-done.1.refs_2_, f32[128,128]{1,0:T(8,128)S(1)} %collective-permute-done.2.refs_3_), custom_call_target="tpu_custom_call" | custom-call | tf_op jit(solution)/shard_map/place/pallas_call | solution.py:225
Async XLA Ops:
  0.6 0.7 copy-start.2
  3.5 63.2 %copy-start = (s32[384,2]{0,1:T(2,128)S(1)}, s32[384,2]{0,1:T(2,128)}, u32[]{:S(2)}) copy-start(s32[384,2]{0,1:T(2,128)} %param.5) | copy-start | bytes 9220
  3.5 63.2 %copy-start.1 = (s32[384,1]{0,1:T(1,128)S(1)}, s32[384,1]{0,1:T(1,128)}, u32[]{:S(2)}) copy-start(s32[384,1]{0,1:T(1,128)} %param.6) | copy-start | bytes 4612
  74.4 5.7 %collective-permute-start = (f32[128,128]{1,0:T(8,128)S(1)}, f32[128,128]{1,0:T(8,128)S(1)}, u32[]{:S(2)}, u32[]{:S(2)}) collective-permute-start(f32[128,128]{1,0:T(8,128)S(1)} %get-tuple-element.7), channel_id=1, source_target_pairs={{0,1},{1,2},{2,3},{3,0},{4,5},{5,6},{6,7},{7,4},{8,9},{9,10},{10,1... | collective-permute-start | bytes 196616 | tf_op jit(solution)/shard_map/ppermute | solution.py:222
  75.9 5.8 %collective-permute-start.1 = (f32[128,128]{1,0:T(8,128)S(1)}, f32[128,128]{1,0:T(8,128)S(1)}, u32[]{:S(2)}, u32[]{:S(2)}) collective-permute-start(f32[128,128]{1,0:T(8,128)S(1)} %get-tuple-element.8), channel_id=1, source_target_pairs={{0,2},{1,3},{2,0},{3,1},{4,6},{5,7},{6,4},{7,5},{8,10},{9,11},{10,... | collective-permute-start | bytes 196616 | tf_op jit(solution)/shard_map/ppermute | solution.py:222
  78.7 4.3 %collective-permute-start.2 = (f32[128,128]{1,0:T(8,128)S(1)}, f32[128,128]{1,0:T(8,128)S(1)}, u32[]{:S(2)}, u32[]{:S(2)}) collective-permute-start(f32[128,128]{1,0:T(8,128)S(1)} %get-tuple-element.9), channel_id=1, source_target_pairs={{0,3},{1,0},{2,1},{3,2},{4,7},{5,4},{6,5},{7,6},{8,11},{9,8},{10,9... | collective-permute-start | bytes 196616 | tf_op jit(solution)/shard_map/ppermute | solution.py:222

commit v5 on v4

--- a/solution.py
+++ b/solution.py
@@ -54,17 +54,19 @@
         pltpu.make_async_copy(held.at[at], held.at[at], in_sem.at[c]).wait()
 
 
-def terms_kernel(pairs_sm, data_ref, pairs_ref, groups_ref, *refs):
-    out_refs, (wide, norm, gamma, chosen_ref, rhs_ref) = refs[:-5], refs[-5:]
+def terms_kernel(data_ref, pairs_ref, groups_ref, *refs):
+    out_refs, (wide, norm, gamma, chosen_ref, rhs_ref, pairs_sm, sem) = refs[:-7], refs[-7:]
+    pairs_copy = pltpu.make_async_copy(pairs_ref, pairs_sm, sem)
+    pairs_copy.start()
     n_epochs = data_ref.shape[0]
     n_pairs = pairs_ref.shape[1]
     step = wide.shape[0]
     sub = lax.broadcasted_iota(jnp.int32, (8, LANES), 0)
     lane = lax.broadcasted_iota(jnp.int32, (8, LANES), 1)
     first = sub < 4
-    rows_i = lax.broadcasted_iota(jnp.int32, (LANES, LANES), 0)
-    cols_i = lax.broadcasted_iota(jnp.int32, (LANES, LANES), 1)
-    same_look = (rows_i // 16 == cols_i // 16).astype(jnp.bfloat16)
+    rows_i = lax.broadcasted_iota(jnp.int32, (2 * LANES, LANES), 0)
+    cols_i = lax.broadcasted_iota(jnp.int32, (2 * LANES, LANES), 1)
+    same_look = ((rows_i % LANES) // 16 == cols_i // 16).astype(jnp.bfloat16)
 
     @pl.loop(0, n_epochs // step, unroll=4)
     def _(block):
@@ -74,12 +76,23 @@
         im = wide[:, :, pl.ds(1, 16, stride=2), :]
         power = re * re + im * im
         lines = power[:, :, 0:8] + power[:, :, 8:16]
-        lines = lines + pltpu.roll(lines, 4, 2)
-        level = dot_split(lines.reshape(step * 2 * 8, LANES), same_look).reshape(step, 2, 8, LANES)
+        lines = jnp.where(first, lines[:, 0], lines[:, 1]) + pltpu.roll(
+            jnp.where(first, lines[:, 1], lines[:, 0]), 4, 1
+        )
+        lines = lines.reshape(step * 8, LANES)
+        high = lines.astype(jnp.bfloat16)
+        low = (lines - high.astype(jnp.float32)).astype(jnp.bfloat16)
+        level = jnp.dot(
+            jnp.concatenate([high, low], axis=1), same_look, preferred_element_type=jnp.float32
+        ).reshape(step, 8, LANES)
         inv = lax.rsqrt(level * (1.0 / LOOK_PIXELS) + EPS) * 0.125
-        inv = jnp.concatenate([inv, inv], axis=2)
-        norm[at, 0] = re * inv
-        norm[at, 1] = im * inv
+        swapped = pltpu.roll(inv, 4, 1)
+        for k, inv_k in enumerate((jnp.where(first, inv, swapped), jnp.where(first, swapped, inv))):
+            inv_k = jnp.concatenate([inv_k, inv_k], axis=1)
+            norm[at, 0, k] = re[:, k] * inv_k
+            norm[at, 1, k] = im[:, k] * inv_k
+
+    pairs_copy.wait()
 
     @pl.loop(0, n_pairs // BATCH, unroll=8)
     def _(batch):
@@ -138,8 +151,15 @@
     half = n_pairs // 4
     slot = jnp.where(rank < half, groups * half + rank, n_pairs + groups * half + rank - half)
     hit = (lax.broadcasted_iota(jnp.int32, (2 * n_pairs, n_pairs), 0) == slot).astype(jnp.bfloat16)
-    chosen = split_dot(hit, weight)
-    chosen_ref[...] = jnp.where(comp0, chosen[:n_pairs], chosen[n_pairs:])
+    high = weight.astype(jnp.bfloat16).astype(jnp.float32)
+    middle = (weight - high).astype(jnp.bfloat16).astype(jnp.float32)
+    three = jnp.concatenate([jnp.where(comp0, high, middle), (weight - high) - middle], axis=1)
+    chosen = jnp.dot(hit, three.astype(jnp.bfloat16), preferred_element_type=jnp.float32)
+    first_half = chosen[:n_pairs, :LANES] + pltpu.roll(chosen[:n_pairs, :LANES], LANES - 8, 1)
+    last_half = chosen[n_pairs:, :LANES] + pltpu.roll(chosen[n_pairs:, :LANES], 8, 1)
+    chosen_ref[...] = jnp.where(
+        comp0, first_half + chosen[:n_pairs, LANES:], last_half + chosen[n_pairs:, LANES:]
+    )
     n_members = len(out_refs)
     half, e_out = n_pairs // n_members, n_epochs // n_members
     me = lax.axis_index("pair")
@@ -203,10 +223,10 @@
     data = data.reshape(n_epochs, tiles_dev, 2, part // LANES, LANES)
     data = jnp.swapaxes(data, 2, 3).reshape(n_epochs, tiles_dev, 2 * part // LANES, LANES)
     rows = n_pairs // 4 + n_epochs // n_pair
-    parts = pl.pallas_call(
+    parts = list(pl.pallas_call(
         terms_kernel,
         out_shape=[jax.ShapeDtypeStruct((rows, LANES), jnp.float32)] * n_pair,
-        in_specs=[scalars, vector, vector, vector],
+        in_specs=[vector, vector, vector],
         out_specs=[vector] * n_pair,
         scratch_shapes=[
             pltpu.VMEM((8, tiles_dev, 32, LANES), jnp.float32),
@@ -214,14 +234,16 @@
             pltpu.VMEM((n_pairs // BATCH, BATCH, LANES), jnp.float32),
             pltpu.VMEM((n_pairs, LANES), jnp.float32),
             pltpu.VMEM((n_epochs, LANES), jnp.float32),
+            pltpu.SMEM(pairs_t.shape, jnp.int32),
+            pltpu.SemaphoreType.DMA,
         ],
         compiler_params=pltpu.CompilerParams(vmem_limit_bytes=40 * 1024 * 1024),
         name="terms",
-    )(pairs_t, data, pairs_t, groups_t)
-    parts = [
-        part_k if k == 0 else lax.ppermute(part_k, "pair", [(i, (i + k) % n_pair) for i in range(n_pair)])
-        for k, part_k in enumerate(parts)
-    ]
+    )(data, pairs_t, groups_t))
+    ring = range(n_pair)
+    for k in sorted(ring, key=lambda k: -min(k, n_pair - k)):
+        if k:
+            parts[k] = lax.ppermute(parts[k], "pair", [(i, (i + k) % n_pair) for i in ring])
     return pl.pallas_call(
         place_kernel,
         out_shape=(

time: 84.4 us -> 83.6 us (level)
    pallas_call x1, Pallas kernels: 7.67 us -> 6.81 us  [local(): pl.pallas_call(terms_kernel, out_shape=[jax.ShapeDtypeStruct((rows, LANES...]
where the time goes in v5:
time: 83.6 us; the launch traced here: 83.3 us
  blocking collectives  63.2 us (76%)
  Pallas kernels  10.3 us (12%)
  starting transfers between devices  5.73 us (7%)
  waiting for transfers between devices  2.84 us (3%)
    all_to_all x1, blocking collectives, local(): lax.all_to_all(ordered, 'tile', split_axis=0, concat_axis=0, tiled=True)  63.2 us
    pallas_call x1, Pallas kernels, local(): pl.pallas_call(terms_kernel, out_shape=[jax.ShapeDtypeStruct((rows, LANES...  6.81 us
    ppermute x3, starting transfers between devices, local(): lax.ppermute(parts[k], 'pair', [(i, (i + k) % n_pair) for i in ring])  5.73 us
    ppermute x3, waiting for transfers between devices, local(): lax.ppermute(parts[k], 'pair', [(i, (i + k) % n_pair) for i in ring])  2.84 us
    pallas_call x1, Pallas kernels, local(): pl.pallas_call(order_kernel, out_shape=jax.ShapeDtypeStruct(out_shape, sl...  2.19 us
  transfers between devices with their start and end apart: 3, of which 2 were waited for; matrix products, arithmetic and copies ran while one was open for 0% of the time, Pallas kernels for 0%

profile of v5, /device:TPU:8, one launch (start us, length us, event | category | flops | bytes accessed | tf_op | source)
XLA Modules:
  0.0 83.3 jit_solution(12900895232968551125)
XLA Ops:
  0.6 0.0 copy-start.2
  0.6 0.6 copy-done.2
  1.3 2.2 %order.1 = bf16[64,2,2,2,2048]{4,3,2,1,0:T(2,128)(2,1)S(1)} custom-call(s32[128]{0:T(128)S(1)} %copy-done.2, bf16[2,128,2,8192]{3,2,1,0:T(2,128)(2,1)} %slc_ref.1), custom_call_target="tpu_custom_call" | custom-call | tf_op jit(solution)/shard_map/order/pallas_call | solution.py:211
  3.5 0.0 copy-start
  3.5 0.0 copy-start.1
  3.5 63.2 %all_to_all.5 = bf16[64,2,2,2,2048]{4,3,2,1,0:T(2,128)(2,1)S(1)} all-to-all(bf16[64,2,2,2,2048]{4,3,2,1,0:T(2,128)(2,1)S(1)} %order.1), channel_id=1, replica_groups=mesh['tile'=64,'pair'=4] {'tile'}, dimensions={0} | all-to-all | bytes 4194304 | tf_op jit(solution)/shard_map/all_to_all | solution.py:222
  66.7 0.0 copy-done
  66.7 0.0 copy-done.1
  66.7 6.8 %terms.1 = (f32[128,128]{1,0:T(8,128)S(1)}, f32[128,128]{1,0:T(8,128)S(1)}, f32[128,128]{1,0:T(8,128)S(1)}, f32[128,128]{1,0:T(8,128)S(1)}) custom-call(bf16[128,2,32,128]{3,2,1,0:T(8,128)(2,1)S(1)} %bitcast.7, s32[2,384]{1,0:T(2,128)S(1)} %bitcast.8, s32[1,384]{1,0:T(1,128)S(1)} %bitcast.9), custom_call_target="tpu_custom_call" | custom-call | tf_op jit(solution)/shard_map/terms/pallas_call | solution.py:226
  73.5 1.6 %collective-permute-start = (f32[128,128]{1,0:T(8,128)S(1)}, f32[128,128]{1,0:T(8,128)S(1)}, u32[]{:S(2)}, u32[]{:S(2)}) collective-permute-start(f32[128,128]{1,0:T(8,128)S(1)} %get-tuple-element.7), channel_id=1, source_target_pairs={{0,1},{1,2},{2,3},{3,0},{4,5},{5,6},{6,7},{7,4},{8,9},{9,10},{10,1... | collective-permute-start | bytes 196616 | tf_op jit(solution)/shard_map/ppermute | solution.py:246
  75.1 2.7 %collective-permute-start.1 = (f32[128,128]{1,0:T(8,128)S(1)}, f32[128,128]{1,0:T(8,128)S(1)}, u32[]{:S(2)}, u32[]{:S(2)}) collective-permute-start(f32[128,128]{1,0:T(8,128)S(1)} %get-tuple-element.8), channel_id=1, source_target_pairs={{0,2},{1,3},{2,0},{3,1},{4,6},{5,7},{6,4},{7,5},{8,10},{9,11},{10,... | collective-permute-start | bytes 196616 | tf_op jit(solution)/shard_map/ppermute | solution.py:246
  77.8 1.4 %collective-permute-start.2 = (f32[128,128]{1,0:T(8,128)S(1)}, f32[128,128]{1,0:T(8,128)S(1)}, u32[]{:S(2)}, u32[]{:S(2)}) collective-permute-start(f32[128,128]{1,0:T(8,128)S(1)} %get-tuple-element.9), channel_id=1, source_target_pairs={{0,3},{1,0},{2,1},{3,2},{4,7},{5,4},{6,5},{7,6},{8,11},{9,8},{10,9... | collective-permute-start | bytes 196616 | tf_op jit(solution)/shard_map/ppermute | solution.py:246
  79.2 0.0 collective-permute-done.refs_1_
  79.2 1.6 %collective-permute-done.1.refs_2_ = f32[128,128]{1,0:T(8,128)S(1)} collective-permute-done((f32[128,128]{1,0:T(8,128)S(1)}, f32[128,128]{1,0:T(8,128)S(1)}, u32[]{:S(2)}, u32[]{:S(2)}) %collective-permute-start.1) | collective-permute-done | bytes 65568 | tf_op jit(solution)/shard_map/ppermute | solution.py:246
  80.8 1.2 %collective-permute-done.2.refs_3_ = f32[128,128]{1,0:T(8,128)S(1)} collective-permute-done((f32[128,128]{1,0:T(8,128)S(1)}, f32[128,128]{1,0:T(8,128)S(1)}, u32[]{:S(2)}, u32[]{:S(2)}) %collective-permute-start.2) | collective-permute-done | bytes 65568 | tf_op jit(solution)/shard_map/ppermute | solution.py:246
  82.1 1.3 %place.1 = (f32[32,2,2,128]{3,2,1,0:T(2,128)}, f32[192,2,128]{2,1,0:T(2,128)}) custom-call(f32[128,128]{1,0:T(8,128)S(1)} %get-tuple-element.6.refs_0_, f32[128,128]{1,0:T(8,128)S(1)} %collective-permute-done.refs_1_, f32[128,128]{1,0:T(8,128)S(1)} %collective-permute-done.1.refs_2_, f32[128,128]{1,0:T(8,128)S(1)} %collective-permute-done.2.refs_3_), custom_call_target="tpu_custom_call" | custom-call | tf_op jit(solution)/shard_map/place/pallas_call | solution.py:247
Async XLA Ops:
  0.6 0.7 copy-start.2
  3.5 63.2 %copy-start = (s32[384,2]{0,1:T(2,128)S(1)}, s32[384,2]{0,1:T(2,128)}, u32[]{:S(2)}) copy-start(s32[384,2]{0,1:T(2,128)} %param.5) | copy-start | bytes 9220
  3.5 63.2 %copy-start.1 = (s32[384,1]{0,1:T(1,128)S(1)}, s32[384,1]{0,1:T(1,128)}, u32[]{:S(2)}) copy-start(s32[384,1]{0,1:T(1,128)} %param.6) | copy-start | bytes 4612
  73.5 5.7 %collective-permute-start = (f32[128,128]{1,0:T(8,128)S(1)}, f32[128,128]{1,0:T(8,128)S(1)}, u32[]{:S(2)}, u32[]{:S(2)}) collective-permute-start(f32[128,128]{1,0:T(8,128)S(1)} %get-tuple-element.7), channel_id=1, source_target_pairs={{0,1},{1,2},{2,3},{3,0},{4,5},{5,6},{6,7},{7,4},{8,9},{9,10},{10,1... | collective-permute-start | bytes 196616 | tf_op jit(solution)/shard_map/ppermute | solution.py:246
  75.1 5.8 %collective-permute-start.1 = (f32[128,128]{1,0:T(8,128)S(1)}, f32[128,128]{1,0:T(8,128)S(1)}, u32[]{:S(2)}, u32[]{:S(2)}) collective-permute-start(f32[128,128]{1,0:T(8,128)S(1)} %get-tuple-element.8), channel_id=1, source_target_pairs={{0,2},{1,3},{2,0},{3,1},{4,6},{5,7},{6,4},{7,5},{8,10},{9,11},{10,... | collective-permute-start | bytes 196616 | tf_op jit(solution)/shard_map/ppermute | solution.py:246
  77.8 4.3 %collective-permute-start.2 = (f32[128,128]{1,0:T(8,128)S(1)}, f32[128,128]{1,0:T(8,128)S(1)}, u32[]{:S(2)}, u32[]{:S(2)}) collective-permute-start(f32[128,128]{1,0:T(8,128)S(1)} %get-tuple-element.9), channel_id=1, source_target_pairs={{0,3},{1,0},{2,1},{3,2},{4,7},{5,4},{6,5},{7,6},{8,11},{9,8},{10,9... | collective-permute-start | bytes 196616 | tf_op jit(solution)/shard_map/ppermute | solution.py:246

commit v6 on v5

--- a/solution.py
+++ b/solution.py
@@ -23,14 +23,8 @@
     return out[:, :width] + out[:, width : 2 * width] + out[:, 2 * width :]
 
 
-def dot_split(x, ones):
-    high = x.astype(jnp.bfloat16)
-    rest = x - high.astype(jnp.float32)
-    middle = rest.astype(jnp.bfloat16)
-    low = (rest - middle.astype(jnp.float32)).astype(jnp.bfloat16)
-    rows = x.shape[0]
-    out = jnp.dot(jnp.concatenate([high, middle, low], axis=0), ones, preferred_element_type=jnp.float32)
-    return out[:rows] + out[rows : 2 * rows] + out[2 * rows :]
+def across(x, lanes):
+    return jnp.take_along_axis(x, lanes, axis=x.ndim - 1, mode="promise_in_bounds")
 
 
 def order_kernel(source_ref, slc_ref, held, in_sem):
@@ -68,7 +62,7 @@
     cols_i = lax.broadcasted_iota(jnp.int32, (2 * LANES, LANES), 1)
     same_look = ((rows_i % LANES) // 16 == cols_i // 16).astype(jnp.bfloat16)
 
-    @pl.loop(0, n_epochs // step, unroll=4)
+    @pl.loop(0, n_epochs // step, unroll=8)
     def _(block):
         at = pl.ds(block * step, step)
         wide[...] = data_ref[at].astype(jnp.float32)
@@ -110,9 +104,8 @@
             return merge(parts[0], parts[1], 8)
 
         def merge(a, b, k):
-            return jnp.where(
-                (lane & k) == 0, a + pltpu.roll(a, LANES - k, 1), b + pltpu.roll(b, k, 1)
-            )
+            own = (lane & k) == 0
+            return jnp.where(own, a, b) + across(jnp.where(own, b, a), lane ^ k)
 
         def tree(js, k):
             if len(js) == 1:
@@ -126,10 +119,10 @@
     sub = lax.broadcasted_iota(jnp.int32, z.shape, 1)
     lane = lax.broadcasted_iota(jnp.int32, z.shape, 2)
     for k in (4, 2, 1):
-        up = pltpu.roll(pltpu.roll(z, k, 2), 8 - k, 1)
-        down = pltpu.roll(pltpu.roll(z, LANES - k, 2), k, 1)
-        low_row, low_lane = (sub & k) == 0, (lane & k) == 0
-        z = jnp.where(low_row == low_lane, z, jnp.where(low_row, up, down))
+        low_row = (sub & k) == 0
+        moved = across(z.reshape(n_pairs, LANES), (lane ^ k).reshape(n_pairs, LANES)).reshape(z.shape)
+        up, down = pltpu.roll(moved, 8 - k, 1), pltpu.roll(moved, k, 1)
+        z = jnp.where(low_row == ((lane & k) == 0), z, jnp.where(low_row, up, down))
     z = z.reshape(n_pairs, LANES)
     comp0 = (lax.broadcasted_iota(jnp.int32, z.shape, 1) & 8) == 0
     square = z * z
@@ -176,18 +169,16 @@
     half = coherence_ref.shape[0] // 2
     width = LANES // n_members
     me = lax.axis_index("pair")
-    i = lax.broadcasted_iota(jnp.int32, (LANES, LANES), 0)
-    j = lax.broadcasted_iota(jnp.int32, (LANES, LANES), 1)
-    ones = (j == (i % 16) * 8 + i // 16).astype(jnp.bfloat16)
-    parts = dot_split(jnp.concatenate([r[...] for r in part_refs], axis=0), ones)
-    owner = lax.broadcasted_iota(jnp.int32, (rows, LANES), 1) // width
+    lane = lax.broadcasted_iota(jnp.int32, (rows, LANES), 1)
+    look = lane % width
+    source = (look % 8) * 16 + look // 8
+    owner = lane // width
     total = [None] * 4
-    for k in range(n_members):
-        member = lax.rem(me + n_members - k, n_members)
-        own = owner == member
-        base = pltpu.roll(parts[k * rows : (k + 1) * rows], member * width, 1)
+    for k, part_ref in enumerate(part_refs):
+        own = owner == lax.rem(me + n_members - k, n_members)
+        part = part_ref[...]
         for g in range(4):
-            piece = base if g == 0 else pltpu.roll(base, LANES - g * width, 1)
+            piece = across(part, source + 4 * g)
             total[g] = piece if k == 0 else jnp.where(own, piece, total[g])
     for comp in range(2):
         for slot in range(2):

time: 83.6 us -> 82.6 us (0.988)
  Pallas kernels: 10.3 us -> 9.31 us
where the time goes in v6:
time: 82.6 us; the launch traced here: 82.4 us
  blocking collectives  63.2 us (77%)
  Pallas kernels  9.31 us (11%)
  starting transfers between devices  5.74 us (7%)
  waiting for transfers between devices  2.83 us (3%)
    all_to_all x1, blocking collectives, local(): lax.all_to_all(ordered, 'tile', split_axis=0, concat_axis=0, tiled=True)  63.2 us
    pallas_call x1, Pallas kernels, local(): pl.pallas_call(terms_kernel, out_shape=[jax.ShapeDtypeStruct((rows, LANES...  6 us
    ppermute x3, starting transfers between devices, local(): lax.ppermute(parts[k], 'pair', [(i, (i + k) % n_pair) for i in ring])  5.74 us
    ppermute x3, waiting for transfers between devices, local(): lax.ppermute(parts[k], 'pair', [(i, (i + k) % n_pair) for i in ring])  2.83 us
    pallas_call x1, Pallas kernels, local(): pl.pallas_call(order_kernel, out_shape=jax.ShapeDtypeStruct(out_shape, sl...  2.19 us
  transfers between devices with their start and end apart: 3, of which 2 were waited for; matrix products, arithmetic and copies ran while one was open for 0% of the time, Pallas kernels for 0%

profile of v6, /device:TPU:8, one launch (start us, length us, event | category | flops | bytes accessed | tf_op | source)
XLA Modules:
  0.0 82.4 jit_solution(9692359034823467017)
XLA Ops:
  0.6 0.0 copy-start.2
  0.6 0.6 copy-done.2
  1.3 2.2 %order.1 = bf16[64,2,2,2,2048]{4,3,2,1,0:T(2,128)(2,1)S(1)} custom-call(s32[128]{0:T(128)S(1)} %copy-done.2, bf16[2,128,2,8192]{3,2,1,0:T(2,128)(2,1)} %slc_ref.1), custom_call_target="tpu_custom_call" | custom-call | tf_op jit(solution)/shard_map/order/pallas_call | solution.py:202
  3.5 0.0 copy-start
  3.5 0.0 copy-start.1
  3.5 63.2 %all_to_all.5 = bf16[64,2,2,2,2048]{4,3,2,1,0:T(2,128)(2,1)S(1)} all-to-all(bf16[64,2,2,2,2048]{4,3,2,1,0:T(2,128)(2,1)S(1)} %order.1), channel_id=1, replica_groups=mesh['tile'=64,'pair'=4] {'tile'}, dimensions={0} | all-to-all | bytes 4194304 | tf_op jit(solution)/shard_map/all_to_all | solution.py:213
  66.7 0.0 copy-done
  66.7 0.0 copy-done.1
  66.7 6.0 %terms.1 = (f32[128,128]{1,0:T(8,128)S(1)}, f32[128,128]{1,0:T(8,128)S(1)}, f32[128,128]{1,0:T(8,128)S(1)}, f32[128,128]{1,0:T(8,128)S(1)}) custom-call(bf16[128,2,32,128]{3,2,1,0:T(8,128)(2,1)S(1)} %bitcast.7, s32[2,384]{1,0:T(2,128)S(1)} %bitcast.8, s32[1,384]{1,0:T(1,128)S(1)} %bitcast.9), custom_call_target="tpu_custom_call" | custom-call | tf_op jit(solution)/shard_map/terms/pallas_call | solution.py:217
  72.7 1.6 %collective-permute-start = (f32[128,128]{1,0:T(8,128)S(1)}, f32[128,128]{1,0:T(8,128)S(1)}, u32[]{:S(2)}, u32[]{:S(2)}) collective-permute-start(f32[128,128]{1,0:T(8,128)S(1)} %get-tuple-element.7), channel_id=1, source_target_pairs={{0,1},{1,2},{2,3},{3,0},{4,5},{5,6},{6,7},{7,4},{8,9},{9,10},{10,1... | collective-permute-start | bytes 196616 | tf_op jit(solution)/shard_map/ppermute | solution.py:237
  74.3 2.7 %collective-permute-start.1 = (f32[128,128]{1,0:T(8,128)S(1)}, f32[128,128]{1,0:T(8,128)S(1)}, u32[]{:S(2)}, u32[]{:S(2)}) collective-permute-start(f32[128,128]{1,0:T(8,128)S(1)} %get-tuple-element.8), channel_id=1, source_target_pairs={{0,2},{1,3},{2,0},{3,1},{4,6},{5,7},{6,4},{7,5},{8,10},{9,11},{10,... | collective-permute-start | bytes 196616 | tf_op jit(solution)/shard_map/ppermute | solution.py:237
  77.0 1.4 %collective-permute-start.2 = (f32[128,128]{1,0:T(8,128)S(1)}, f32[128,128]{1,0:T(8,128)S(1)}, u32[]{:S(2)}, u32[]{:S(2)}) collective-permute-start(f32[128,128]{1,0:T(8,128)S(1)} %get-tuple-element.9), channel_id=1, source_target_pairs={{0,3},{1,0},{2,1},{3,2},{4,7},{5,4},{6,5},{7,6},{8,11},{9,8},{10,9... | collective-permute-start | bytes 196616 | tf_op jit(solution)/shard_map/ppermute | solution.py:237
  78.4 0.0 collective-permute-done.refs_1_
  78.4 1.6 %collective-permute-done.1.refs_2_ = f32[128,128]{1,0:T(8,128)S(1)} collective-permute-done((f32[128,128]{1,0:T(8,128)S(1)}, f32[128,128]{1,0:T(8,128)S(1)}, u32[]{:S(2)}, u32[]{:S(2)}) %collective-permute-start.1) | collective-permute-done | bytes 65568 | tf_op jit(solution)/shard_map/ppermute | solution.py:237
  80.0 1.2 %collective-permute-done.2.refs_3_ = f32[128,128]{1,0:T(8,128)S(1)} collective-permute-done((f32[128,128]{1,0:T(8,128)S(1)}, f32[128,128]{1,0:T(8,128)S(1)}, u32[]{:S(2)}, u32[]{:S(2)}) %collective-permute-start.2) | collective-permute-done | bytes 65568 | tf_op jit(solution)/shard_map/ppermute | solution.py:237
  81.3 1.1 %place.1 = (f32[32,2,2,128]{3,2,1,0:T(2,128)}, f32[192,2,128]{2,1,0:T(2,128)}) custom-call(f32[128,128]{1,0:T(8,128)S(1)} %get-tuple-element.6.refs_0_, f32[128,128]{1,0:T(8,128)S(1)} %collective-permute-done.refs_1_, f32[128,128]{1,0:T(8,128)S(1)} %collective-permute-done.1.refs_2_, f32[128,128]{1,0:T(8,128)S(1)} %collective-permute-done.2.refs_3_), custom_call_target="tpu_custom_call" | custom-call | tf_op jit(solution)/shard_map/place/pallas_call | solution.py:238
Async XLA Ops:
  0.6 0.7 copy-start.2
  3.5 63.2 %copy-start = (s32[384,2]{0,1:T(2,128)S(1)}, s32[384,2]{0,1:T(2,128)}, u32[]{:S(2)}) copy-start(s32[384,2]{0,1:T(2,128)} %param.5) | copy-start | bytes 9220
  3.5 63.2 %copy-start.1 = (s32[384,1]{0,1:T(1,128)S(1)}, s32[384,1]{0,1:T(1,128)}, u32[]{:S(2)}) copy-start(s32[384,1]{0,1:T(1,128)} %param.6) | copy-start | bytes 4612
  72.7 5.7 %collective-permute-start = (f32[128,128]{1,0:T(8,128)S(1)}, f32[128,128]{1,0:T(8,128)S(1)}, u32[]{:S(2)}, u32[]{:S(2)}) collective-permute-start(f32[128,128]{1,0:T(8,128)S(1)} %get-tuple-element.7), channel_id=1, source_target_pairs={{0,1},{1,2},{2,3},{3,0},{4,5},{5,6},{6,7},{7,4},{8,9},{9,10},{10,1... | collective-permute-start | bytes 196616 | tf_op jit(solution)/shard_map/ppermute | solution.py:237
  74.3 5.8 %collective-permute-start.1 = (f32[128,128]{1,0:T(8,128)S(1)}, f32[128,128]{1,0:T(8,128)S(1)}, u32[]{:S(2)}, u32[]{:S(2)}) collective-permute-start(f32[128,128]{1,0:T(8,128)S(1)} %get-tuple-element.8), channel_id=1, source_target_pairs={{0,2},{1,3},{2,0},{3,1},{4,6},{5,7},{6,4},{7,5},{8,10},{9,11},{10,... | collective-permute-start | bytes 196616 | tf_op jit(solution)/shard_map/ppermute | solution.py:237
  77.0 4.3 %collective-permute-start.2 = (f32[128,128]{1,0:T(8,128)S(1)}, f32[128,128]{1,0:T(8,128)S(1)}, u32[]{:S(2)}, u32[]{:S(2)}) collective-permute-start(f32[128,128]{1,0:T(8,128)S(1)} %get-tuple-element.9), channel_id=1, source_target_pairs={{0,3},{1,0},{2,1},{3,2},{4,7},{5,4},{6,5},{7,6},{8,11},{9,8},{10,9... | collective-permute-start | bytes 196616 | tf_op jit(solution)/shard_map/ppermute | solution.py:237

commit v7 on v6

--- a/solution.py
+++ b/solution.py
@@ -220,7 +220,7 @@
         in_specs=[vector, vector, vector],
         out_specs=[vector] * n_pair,
         scratch_shapes=[
-            pltpu.VMEM((8, tiles_dev, 32, LANES), jnp.float32),
+            pltpu.VMEM((16, tiles_dev, 32, LANES), jnp.float32),
             pltpu.VMEM((n_epochs, 2, tiles_dev, 16, LANES), jnp.float32),
             pltpu.VMEM((n_pairs // BATCH, BATCH, LANES), jnp.float32),
             pltpu.VMEM((n_pairs, LANES), jnp.float32),

time: 82.6 us -> 82.6 us (level)
  no operation moved by 1% of the time
where the time goes in v7:
time: 82.6 us; the launch traced here: 82.4 us
  blocking collectives  63.2 us (77%)
  Pallas kernels  9.3 us (11%)
  starting transfers between devices  5.73 us (7%)
  waiting for transfers between devices  2.83 us (3%)
    all_to_all x1, blocking collectives, local(): lax.all_to_all(ordered, 'tile', split_axis=0, concat_axis=0, tiled=True)  63.2 us
    pallas_call x1, Pallas kernels, local(): pl.pallas_call(terms_kernel, out_shape=[jax.ShapeDtypeStruct((rows, LANES...  6 us
    ppermute x3, starting transfers between devices, local(): lax.ppermute(parts[k], 'pair', [(i, (i + k) % n_pair) for i in ring])  5.73 us
    ppermute x3, waiting for transfers between devices, local(): lax.ppermute(parts[k], 'pair', [(i, (i + k) % n_pair) for i in ring])  2.83 us
    pallas_call x1, Pallas kernels, local(): pl.pallas_call(order_kernel, out_shape=jax.ShapeDtypeStruct(out_shape, sl...  2.19 us
  transfers between devices with their start and end apart: 3, of which 2 were waited for; matrix products, arithmetic and copies ran while one was open for 0% of the time, Pallas kernels for 0%

profile of v7, /device:TPU:8, one launch (start us, length us, event | category | flops | bytes accessed | tf_op | source)
XLA Modules:
  0.0 82.4 jit_solution(13894483204962173977)
XLA Ops:
  0.6 0.0 copy-start.2
  0.6 0.6 copy-done.2
  1.3 2.2 %order.1 = bf16[64,2,2,2,2048]{4,3,2,1,0:T(2,128)(2,1)S(1)} custom-call(s32[128]{0:T(128)S(1)} %copy-done.2, bf16[2,128,2,8192]{3,2,1,0:T(2,128)(2,1)} %slc_ref.1), custom_call_target="tpu_custom_call" | custom-call | tf_op jit(solution)/shard_map/order/pallas_call | solution.py:202
  3.5 0.0 copy-start
  3.5 0.0 copy-start.1
  3.5 63.2 %all_to_all.5 = bf16[64,2,2,2,2048]{4,3,2,1,0:T(2,128)(2,1)S(1)} all-to-all(bf16[64,2,2,2,2048]{4,3,2,1,0:T(2,128)(2,1)S(1)} %order.1), channel_id=1, replica_groups=mesh['tile'=64,'pair'=4] {'tile'}, dimensions={0} | all-to-all | bytes 4194304 | tf_op jit(solution)/shard_map/all_to_all | solution.py:213
  66.7 0.0 copy-done
  66.7 0.0 copy-done.1
  66.7 6.0 %terms.1 = (f32[128,128]{1,0:T(8,128)S(1)}, f32[128,128]{1,0:T(8,128)S(1)}, f32[128,128]{1,0:T(8,128)S(1)}, f32[128,128]{1,0:T(8,128)S(1)}) custom-call(bf16[128,2,32,128]{3,2,1,0:T(8,128)(2,1)S(1)} %bitcast.7, s32[2,384]{1,0:T(2,128)S(1)} %bitcast.8, s32[1,384]{1,0:T(1,128)S(1)} %bitcast.9), custom_call_target="tpu_custom_call" | custom-call | tf_op jit(solution)/shard_map/terms/pallas_call | solution.py:217
  72.7 1.6 %collective-permute-start = (f32[128,128]{1,0:T(8,128)S(1)}, f32[128,128]{1,0:T(8,128)S(1)}, u32[]{:S(2)}, u32[]{:S(2)}) collective-permute-start(f32[128,128]{1,0:T(8,128)S(1)} %get-tuple-element.7), channel_id=1, source_target_pairs={{0,1},{1,2},{2,3},{3,0},{4,5},{5,6},{6,7},{7,4},{8,9},{9,10},{10,1... | collective-permute-start | bytes 196616 | tf_op jit(solution)/shard_map/ppermute | solution.py:237
  74.3 2.7 %collective-permute-start.1 = (f32[128,128]{1,0:T(8,128)S(1)}, f32[128,128]{1,0:T(8,128)S(1)}, u32[]{:S(2)}, u32[]{:S(2)}) collective-permute-start(f32[128,128]{1,0:T(8,128)S(1)} %get-tuple-element.8), channel_id=1, source_target_pairs={{0,2},{1,3},{2,0},{3,1},{4,6},{5,7},{6,4},{7,5},{8,10},{9,11},{10,... | collective-permute-start | bytes 196616 | tf_op jit(solution)/shard_map/ppermute | solution.py:237
  77.0 1.4 %collective-permute-start.2 = (f32[128,128]{1,0:T(8,128)S(1)}, f32[128,128]{1,0:T(8,128)S(1)}, u32[]{:S(2)}, u32[]{:S(2)}) collective-permute-start(f32[128,128]{1,0:T(8,128)S(1)} %get-tuple-element.9), channel_id=1, source_target_pairs={{0,3},{1,0},{2,1},{3,2},{4,7},{5,4},{6,5},{7,6},{8,11},{9,8},{10,9... | collective-permute-start | bytes 196616 | tf_op jit(solution)/shard_map/ppermute | solution.py:237
  78.4 0.0 collective-permute-done.refs_1_
  78.4 1.6 %collective-permute-done.1.refs_2_ = f32[128,128]{1,0:T(8,128)S(1)} collective-permute-done((f32[128,128]{1,0:T(8,128)S(1)}, f32[128,128]{1,0:T(8,128)S(1)}, u32[]{:S(2)}, u32[]{:S(2)}) %collective-permute-start.1) | collective-permute-done | bytes 65568 | tf_op jit(solution)/shard_map/ppermute | solution.py:237
  80.0 1.2 %collective-permute-done.2.refs_3_ = f32[128,128]{1,0:T(8,128)S(1)} collective-permute-done((f32[128,128]{1,0:T(8,128)S(1)}, f32[128,128]{1,0:T(8,128)S(1)}, u32[]{:S(2)}, u32[]{:S(2)}) %collective-permute-start.2) | collective-permute-done | bytes 65568 | tf_op jit(solution)/shard_map/ppermute | solution.py:237
  81.3 1.1 %place.1 = (f32[32,2,2,128]{3,2,1,0:T(2,128)}, f32[192,2,128]{2,1,0:T(2,128)}) custom-call(f32[128,128]{1,0:T(8,128)S(1)} %get-tuple-element.6.refs_0_, f32[128,128]{1,0:T(8,128)S(1)} %collective-permute-done.refs_1_, f32[128,128]{1,0:T(8,128)S(1)} %collective-permute-done.1.refs_2_, f32[128,128]{1,0:T(8,128)S(1)} %collective-permute-done.2.refs_3_), custom_call_target="tpu_custom_call" | custom-call | tf_op jit(solution)/shard_map/place/pallas_call | solution.py:238
Async XLA Ops:
  0.6 0.7 copy-start.2
  3.5 63.2 %copy-start = (s32[384,2]{0,1:T(2,128)S(1)}, s32[384,2]{0,1:T(2,128)}, u32[]{:S(2)}) copy-start(s32[384,2]{0,1:T(2,128)} %param.5) | copy-start | bytes 9220
  3.5 63.2 %copy-start.1 = (s32[384,1]{0,1:T(1,128)S(1)}, s32[384,1]{0,1:T(1,128)}, u32[]{:S(2)}) copy-start(s32[384,1]{0,1:T(1,128)} %param.6) | copy-start | bytes 4612
  72.7 5.7 %collective-permute-start = (f32[128,128]{1,0:T(8,128)S(1)}, f32[128,128]{1,0:T(8,128)S(1)}, u32[]{:S(2)}, u32[]{:S(2)}) collective-permute-start(f32[128,128]{1,0:T(8,128)S(1)} %get-tuple-element.7), channel_id=1, source_target_pairs={{0,1},{1,2},{2,3},{3,0},{4,5},{5,6},{6,7},{7,4},{8,9},{9,10},{10,1... | collective-permute-start | bytes 196616 | tf_op jit(solution)/shard_map/ppermute | solution.py:237
  74.3 5.8 %collective-permute-start.1 = (f32[128,128]{1,0:T(8,128)S(1)}, f32[128,128]{1,0:T(8,128)S(1)}, u32[]{:S(2)}, u32[]{:S(2)}) collective-permute-start(f32[128,128]{1,0:T(8,128)S(1)} %get-tuple-element.8), channel_id=1, source_target_pairs={{0,2},{1,3},{2,0},{3,1},{4,6},{5,7},{6,4},{7,5},{8,10},{9,11},{10,... | collective-permute-start | bytes 196616 | tf_op jit(solution)/shard_map/ppermute | solution.py:237
  77.0 4.3 %collective-permute-start.2 = (f32[128,128]{1,0:T(8,128)S(1)}, f32[128,128]{1,0:T(8,128)S(1)}, u32[]{:S(2)}, u32[]{:S(2)}) collective-permute-start(f32[128,128]{1,0:T(8,128)S(1)} %get-tuple-element.9), channel_id=1, source_target_pairs={{0,3},{1,0},{2,1},{3,2},{4,7},{5,4},{6,5},{7,6},{8,11},{9,8},{10,9... | collective-permute-start | bytes 196616 | tf_op jit(solution)/shard_map/ppermute | solution.py:237
